TPU v7x, 128 devices: a whole 4x4x4 slice. The times are simulated.
128 devices in a mesh: ha: 8 (over z, x_lo), wa: 4 (over y), ta: 4 (over x_hi, core).
Axes of the slice: x: 4 (x_hi: 2, x_lo: 2; x = x_hi * 2 + x_lo), y: 4, z: 4, core: 2. Of those that a mesh axis runs over, the one named last changes fastest.
Arguments:
- queries: bfloat16 [12, 32, 64, 3072], P(None, 'wa', 'ha', 'ta'), may hold values from -10 to 10, as said below
- keys_values: bfloat16 [2, 12, 32, 64, 3072], P(None, None, 'wa', 'ha', 'ta'), may hold values from -6 to 6
- out_weight: bfloat16 [3072, 3072], P('ta'), may hold values from -2.5 to 2.5
Outputs:
- projected: bfloat16 [12, 32, 64, 3072], P(None, 'wa', 'ha', 'ta')
Inputs may be any that keep to these rules, and one draw needn't show every extreme that they name: `queries`: query entries.
All inputs are finite; a program needn't handle non-finite values.
Results may differ from a plain program's by a relative error of at most 0.013.
Values may be sent and summed in bfloat16 or wider, within the bound.
No kernel may reach another device: no remote copies, remote signals or barrier semaphores. Data moves between devices by JAX's collectives and lax.ppermute only.
A program may use at most 128 MiB of HBM per device.

v0:
```python
import jax
import jax.numpy as jnp
from jax import lax
from jax.sharding import PartitionSpec as P

HD = 128
TILE_T = 6
TILE_H = 8
TILE_W = 8


def extended_2(cells, sides, width):
    for axis, dim in sides:
        count = lax.axis_size(axis)
        ends = count - 1
        head = lax.slice_in_dim(cells, 0, width, axis=dim)
        tail = lax.slice_in_dim(cells, cells.shape[dim] - width, cells.shape[dim], axis=dim)
        cells = jnp.concatenate(
            [
                lax.ppermute(tail, axis, [(i, (i + 1) % count) for i in range(ends)]),
                cells,
                lax.ppermute(head, axis, [((i + 1) % count, i) for i in range(ends)]),
            ],
            axis=dim,
        )
    return cells


def body(queries, keys_values, out_weight):
    frames, rows, cols, channels = queries.shape
    extended = extended_2(keys_values, (("wa", 2),), TILE_H)
    extended = extended_2(extended, (("ha", 3),), TILE_W)
    all_rows = rows * lax.axis_size("wa")
    all_cols = cols * lax.axis_size("ha")
    first_row = lax.axis_index("wa") * rows
    first_col = lax.axis_index("ha") * cols
    key_span_rows = rows + 2 * TILE_H
    key_span_cols = cols + 2 * TILE_W
    frame_ids = jnp.arange(frames, dtype=jnp.int32)
    query_frame = jnp.broadcast_to(frame_ids[:, None, None], (frames, rows, cols)).reshape(-1)
    query_row = jnp.broadcast_to(
        (first_row + jnp.arange(rows, dtype=jnp.int32))[None, :, None], (frames, rows, cols)
    ).reshape(-1)
    query_col = jnp.broadcast_to(
        (first_col + jnp.arange(cols, dtype=jnp.int32))[None, None, :], (frames, rows, cols)
    ).reshape(-1)
    shape_keys = (frames, key_span_rows, key_span_cols)
    key_frame = jnp.broadcast_to(frame_ids[:, None, None], shape_keys).reshape(-1)
    key_row = jnp.broadcast_to(
        (first_row - TILE_H + jnp.arange(key_span_rows, dtype=jnp.int32))[None, :, None], shape_keys
    ).reshape(-1)
    key_col = jnp.broadcast_to(
        (first_col - TILE_W + jnp.arange(key_span_cols, dtype=jnp.int32))[None, None, :], shape_keys
    ).reshape(-1)
    inside = (key_row >= 0) & (key_row < all_rows) & (key_col >= 0) & (key_col < all_cols)
    allowed = jnp.abs(query_frame[:, None] // TILE_T - key_frame[None, :] // TILE_T) <= 1
    allowed = allowed & (jnp.abs(query_row[:, None] // TILE_H - key_row[None, :] // TILE_H) <= 1)
    allowed = allowed & (jnp.abs(query_col[:, None] // TILE_W - key_col[None, :] // TILE_W) <= 1)
    allowed = allowed & inside[None, :]
    query_flat = queries.reshape(-1, channels)
    keys_flat = extended[0].reshape(-1, channels)
    values_flat = extended[1].reshape(-1, channels)
    heads_here = channels // HD

    def one_head(head):
        start = head * HD
        head_queries = lax.dynamic_slice_in_dim(query_flat, start, HD, 1)
        head_keys = lax.dynamic_slice_in_dim(keys_flat, start, HD, 1)
        head_values = lax.dynamic_slice_in_dim(values_flat, start, HD, 1)
        scores = lax.dot_general(
            head_queries, head_keys, (((1,), (1,)), ((), ())), preferred_element_type=jnp.float32
        ) * HD ** (-0.5)
        scores = jnp.where(allowed, scores, -1e30)
        row_max = jnp.max(scores, axis=1, keepdims=True)
        weights = jnp.where(allowed, jnp.exp(scores - row_max), 0.0)
        row_total = jnp.sum(weights, axis=1, keepdims=True)
        mixed = (
            jnp.dot(weights.astype(jnp.bfloat16), head_values, preferred_element_type=jnp.float32)
            / row_total
        )
        return mixed.astype(jnp.bfloat16)

    attended = lax.map(one_head, jnp.arange(heads_here, dtype=jnp.int32))
    attention = attended.transpose(1, 0, 2).reshape(-1, channels)
    partial_rows = jnp.dot(attention, out_weight, preferred_element_type=jnp.float32)
    partial_rows = partial_rows.astype(jnp.bfloat16).astype(jnp.float32)
    summed = lax.psum_scatter(
        partial_rows.astype(jnp.bfloat16), "ta", scatter_dimension=1, tiled=True
    )
    return summed.reshape(frames, rows, cols, -1)


def solution(mesh):
    return jax.shard_map(
        body,
        mesh=mesh,
        in_specs=(P(None, "wa", "ha", "ta"), P(None, None, "wa", "ha", "ta"), P("ta", None)),
        out_specs=P(None, "wa", "ha", "ta"),
        check_vma=False,
    )
```

profile of v0, /device:TPU:1, one launch (start us, length us, event | category | flops | bytes accessed | tf_op | source)
XLA Modules:
  0.0 839.5 jit_solution(11812223159938282034)
XLA Ops:
  6.5 4.2 collective-permute-start
  10.7 1.3 collective-permute-start.1
  12.0 48.8 %collective-permute-done = bf16[2,12,8,8,768]{4,3,2,1,0:T(8,128)(2,1)S(1)} collective-permute-done((bf16[2,12,8,8,768]{4,3,2,1,0:T(8,128)(2,1)}, bf16[2,12,8,8,768]{4,3,2,1,0:T(8,128)(2,1)S(1)}, u32[]{:S(2)}, u32[]{:S(2)}) %collective-permute-start) | collective-permute-done | bytes 2359328 | tf_op jit(solution)/shard_map/ppermute | solution.py:20
  60.8 1.7 constant_dynamic-update-slice_fusion.3
  62.4 3.3 constant_dynamic-update-slice_fusion.2
  65.7 1.6 constant_dynamic-update-slice_fusion.1
  67.3 6.1 collective-permute-start.2
  76.0 144.8 %collective-permute-done.2 = bf16[2,12,24,8,768]{4,3,2,1,0:T(8,128)(2,1)} collective-permute-done((bf16[2,12,24,8,768]{4,3,2,1,0:T(8,128)(2,1)}, bf16[2,12,24,8,768]{4,3,2,1,0:T(8,128)(2,1)}, u32[]{:S(2)}, u32[]{:S(2)}) %collective-permute-start.2) | collective-permute-done | bytes 7077920 | tf_op jit(solution)/shard_map/ppermute | solution.py:20
  220.9 154.0 %collective-permute-done.3 = bf16[2,12,24,8,768]{4,3,2,1,0:T(8,128)(2,1)} collective-permute-done((bf16[2,12,24,8,768]{4,3,2,1,0:T(8,128)(2,1)}, bf16[2,12,24,8,768]{4,3,2,1,0:T(8,128)(2,1)}, u32[]{:S(2)}, u32[]{:S(2)}) %collective-permute-start.3) | collective-permute-done | bytes 7077920 | tf_op jit(solution)/shard_map/ppermute | solution.py:22
  374.9 9.6 %pad_maximum_fusion = bf16[2,12,24,24,768]{4,3,2,1,0:T(8,128)(2,1)S(1)} fusion(bf16[2,12,24,8,768]{4,3,2,1,0:T(8,128)(2,1)} %collective-permute-done.3, bf16[2,12,24,8,768]{4,3,2,1,0:T(8,128)(2,1)} %constant_dynamic-update-slice_fusion.1, bf16[2,12,24,8,768]{4,3,2,1,0:T(8,128)(2,1)} %collective-permute-done.2), kind=kLoop, calls=%fused_computation.26 | loop fusion | flops 63700992 | bytes 42467328 | tf_op jit(solution)/shard_map/concatenate | solution.py:18
  384.5 7.5 fusion.49
  392.0 373.1 %while.11 = (s32[]{:T(128)}, bf16[6,768,128]{1,2,0:T(8,128)(2,1)S(1)}, s32[6]{0:T(128)S(1)}, bf16[768,768]{1,0:T(8,128)(2,1)}, bf16[6912,768]{1,0:T(8,128)(2,1)}...) while((s32[]{:T(128)}, ...), condition=%wide.region_3.4_spmd.clone, body=%wide.region_0.3_spmd.clone.sunk | while | flops 2978216448 | bytes 68733408 | solution.py:83
  393.3 18.5 %fusion.59 = (f32[768]{0:T(1024)S(1)}, f32[768,6912]{1,0:T(8,128)S(1)}) fusion(pred[6912]{0:T(1024)(128)(4,1)S(1)} %get-tuple-element.241, s32[6912]{0:T(1024)S(1)} %get-tuple-element.239, s32[768]{0:T(1024)S(1)} %get-tuple-element.240, s32[6912]{0:T(1024)S(1)} %get-tuple-element.237, s32[768]{0:T(1024)S(1)} %get-tuple-element.238, ...), kind=kOutput, calls=%fused_computation.9.clone.1 | convolution fusion | flops 1438579968 | bytes 23302912 | tf_op jit(solution)/shard_map/while/body/eval_jaxpr/dot_general | solution.py:70
  411.7 20.3 %fusion.60 = f32[768]{0:T(1024)S(1)} fusion(f32[768,6912]{1,0:T(8,128)S(1)} %get-tuple-element.193, f32[768]{0:T(1024)S(1)} %get-tuple-element.194, pred[6912]{0:T(1024)(128)(4,1)S(1)} %get-tuple-element.241, s32[6912]{0:T(1024)S(1)} %get-tuple-element.239, s32[768]{0:T(1024)S(1)} %get-tuple-element.240, s32[6912]{0:T(1024)S(1)} %get-tuple-element.237, ...), kind=kLoop, calls=%fused_computation.10.clone.1 | loop fusion | flops 90242304 | bytes 21338880 | tf_op jit(solution)/shard_map/while/body/eval_jaxpr/reduce_sum | solution.py:76
  432.1 19.5 %fusion.61 = bf16[1,768,128]{2,1,0:T(8,128)(2,1)S(1)} fusion(bf16[6912,768]{1,0:T(8,128)(2,1)} %get-tuple-element.234, s32[]{:T(128)S(6)} %select_n.118, f32[768,6912]{1,0:T(8,128)S(1)} %get-tuple-element.193, f32[768]{0:T(1024)S(1)} %get-tuple-element.194, f32[768]{0:T(1024)S(1)} %fusion.60, s32[6912]{0:T(1024)S(1)} %get-tuple-element.239, ...), kind=kOutput, calls=%fused_computation.18.clone.1 | convolution fusion | flops 1449394176 | bytes 23304964 | tf_op jit(solution)/shard_map/while/body/eval_jaxpr/dot_general | solution.py:78
  455.3 18.1 %fusion.59 = (f32[768]{0:T(1024)S(1)}, f32[768,6912]{1,0:T(8,128)S(1)}) fusion(pred[6912]{0:T(1024)(128)(4,1)S(1)} %get-tuple-element.241, s32[6912]{0:T(1024)S(1)} %get-tuple-element.239, s32[768]{0:T(1024)S(1)} %get-tuple-element.240, s32[6912]{0:T(1024)S(1)} %get-tuple-element.237, s32[768]{0:T(1024)S(1)} %get-tuple-element.238, ...), kind=kOutput, calls=%fused_computation.9.clone.1 | convolution fusion | flops 1438579968 | bytes 23302912 | tf_op jit(solution)/shard_map/while/body/eval_jaxpr/dot_general | solution.py:70
  473.5 20.4 %fusion.60 = f32[768]{0:T(1024)S(1)} fusion(f32[768,6912]{1,0:T(8,128)S(1)} %get-tuple-element.193, f32[768]{0:T(1024)S(1)} %get-tuple-element.194, pred[6912]{0:T(1024)(128)(4,1)S(1)} %get-tuple-element.241, s32[6912]{0:T(1024)S(1)} %get-tuple-element.239, s32[768]{0:T(1024)S(1)} %get-tuple-element.240, s32[6912]{0:T(1024)S(1)} %get-tuple-element.237, ...), kind=kLoop, calls=%fused_computation.10.clone.1 | loop fusion | flops 90242304 | bytes 21338880 | tf_op jit(solution)/shard_map/while/body/eval_jaxpr/reduce_sum | solution.py:76
  493.9 19.7 %fusion.61 = bf16[1,768,128]{2,1,0:T(8,128)(2,1)S(1)} fusion(bf16[6912,768]{1,0:T(8,128)(2,1)} %get-tuple-element.234, s32[]{:T(128)S(6)} %select_n.118, f32[768,6912]{1,0:T(8,128)S(1)} %get-tuple-element.193, f32[768]{0:T(1024)S(1)} %get-tuple-element.194, f32[768]{0:T(1024)S(1)} %fusion.60, s32[6912]{0:T(1024)S(1)} %get-tuple-element.239, ...), kind=kOutput, calls=%fused_computation.18.clone.1 | convolution fusion | flops 1449394176 | bytes 23304964 | tf_op jit(solution)/shard_map/while/body/eval_jaxpr/dot_general | solution.py:78
  517.1 18.2 %fusion.59 = (f32[768]{0:T(1024)S(1)}, f32[768,6912]{1,0:T(8,128)S(1)}) fusion(pred[6912]{0:T(1024)(128)(4,1)S(1)} %get-tuple-element.241, s32[6912]{0:T(1024)S(1)} %get-tuple-element.239, s32[768]{0:T(1024)S(1)} %get-tuple-element.240, s32[6912]{0:T(1024)S(1)} %get-tuple-element.237, s32[768]{0:T(1024)S(1)} %get-tuple-element.238, ...), kind=kOutput, calls=%fused_computation.9.clone.1 | convolution fusion | flops 1438579968 | bytes 23302912 | tf_op jit(solution)/shard_map/while/body/eval_jaxpr/dot_general | solution.py:70
  535.3 20.6 %fusion.60 = f32[768]{0:T(1024)S(1)} fusion(f32[768,6912]{1,0:T(8,128)S(1)} %get-tuple-element.193, f32[768]{0:T(1024)S(1)} %get-tuple-element.194, pred[6912]{0:T(1024)(128)(4,1)S(1)} %get-tuple-element.241, s32[6912]{0:T(1024)S(1)} %get-tuple-element.239, s32[768]{0:T(1024)S(1)} %get-tuple-element.240, s32[6912]{0:T(1024)S(1)} %get-tuple-element.237, ...), kind=kLoop, calls=%fused_computation.10.clone.1 | loop fusion | flops 90242304 | bytes 21338880 | tf_op jit(solution)/shard_map/while/body/eval_jaxpr/reduce_sum | solution.py:76
  555.8 19.4 %fusion.61 = bf16[1,768,128]{2,1,0:T(8,128)(2,1)S(1)} fusion(bf16[6912,768]{1,0:T(8,128)(2,1)} %get-tuple-element.234, s32[]{:T(128)S(6)} %select_n.118, f32[768,6912]{1,0:T(8,128)S(1)} %get-tuple-element.193, f32[768]{0:T(1024)S(1)} %get-tuple-element.194, f32[768]{0:T(1024)S(1)} %fusion.60, s32[6912]{0:T(1024)S(1)} %get-tuple-element.239, ...), kind=kOutput, calls=%fused_computation.18.clone.1 | convolution fusion | flops 1449394176 | bytes 23304964 | tf_op jit(solution)/shard_map/while/body/eval_jaxpr/dot_general | solution.py:78
  578.9 18.4 %fusion.59 = (f32[768]{0:T(1024)S(1)}, f32[768,6912]{1,0:T(8,128)S(1)}) fusion(pred[6912]{0:T(1024)(128)(4,1)S(1)} %get-tuple-element.241, s32[6912]{0:T(1024)S(1)} %get-tuple-element.239, s32[768]{0:T(1024)S(1)} %get-tuple-element.240, s32[6912]{0:T(1024)S(1)} %get-tuple-element.237, s32[768]{0:T(1024)S(1)} %get-tuple-element.238, ...), kind=kOutput, calls=%fused_computation.9.clone.1 | convolution fusion | flops 1438579968 | bytes 23302912 | tf_op jit(solution)/shard_map/while/body/eval_jaxpr/dot_general | solution.py:70
  597.2 20.3 %fusion.60 = f32[768]{0:T(1024)S(1)} fusion(f32[768,6912]{1,0:T(8,128)S(1)} %get-tuple-element.193, f32[768]{0:T(1024)S(1)} %get-tuple-element.194, pred[6912]{0:T(1024)(128)(4,1)S(1)} %get-tuple-element.241, s32[6912]{0:T(1024)S(1)} %get-tuple-element.239, s32[768]{0:T(1024)S(1)} %get-tuple-element.240, s32[6912]{0:T(1024)S(1)} %get-tuple-element.237, ...), kind=kLoop, calls=%fused_computation.10.clone.1 | loop fusion | flops 90242304 | bytes 21338880 | tf_op jit(solution)/shard_map/while/body/eval_jaxpr/reduce_sum | solution.py:76
  617.6 19.5 %fusion.61 = bf16[1,768,128]{2,1,0:T(8,128)(2,1)S(1)} fusion(bf16[6912,768]{1,0:T(8,128)(2,1)} %get-tuple-element.234, s32[]{:T(128)S(6)} %select_n.118, f32[768,6912]{1,0:T(8,128)S(1)} %get-tuple-element.193, f32[768]{0:T(1024)S(1)} %get-tuple-element.194, f32[768]{0:T(1024)S(1)} %fusion.60, s32[6912]{0:T(1024)S(1)} %get-tuple-element.239, ...), kind=kOutput, calls=%fused_computation.18.clone.1 | convolution fusion | flops 1449394176 | bytes 23304964 | tf_op jit(solution)/shard_map/while/body/eval_jaxpr/dot_general | solution.py:78
  640.8 18.1 %fusion.59 = (f32[768]{0:T(1024)S(1)}, f32[768,6912]{1,0:T(8,128)S(1)}) fusion(pred[6912]{0:T(1024)(128)(4,1)S(1)} %get-tuple-element.241, s32[6912]{0:T(1024)S(1)} %get-tuple-element.239, s32[768]{0:T(1024)S(1)} %get-tuple-element.240, s32[6912]{0:T(1024)S(1)} %get-tuple-element.237, s32[768]{0:T(1024)S(1)} %get-tuple-element.238, ...), kind=kOutput, calls=%fused_computation.9.clone.1 | convolution fusion | flops 1438579968 | bytes 23302912 | tf_op jit(solution)/shard_map/while/body/eval_jaxpr/dot_general | solution.py:70
  658.9 20.4 %fusion.60 = f32[768]{0:T(1024)S(1)} fusion(f32[768,6912]{1,0:T(8,128)S(1)} %get-tuple-element.193, f32[768]{0:T(1024)S(1)} %get-tuple-element.194, pred[6912]{0:T(1024)(128)(4,1)S(1)} %get-tuple-element.241, s32[6912]{0:T(1024)S(1)} %get-tuple-element.239, s32[768]{0:T(1024)S(1)} %get-tuple-element.240, s32[6912]{0:T(1024)S(1)} %get-tuple-element.237, ...), kind=kLoop, calls=%fused_computation.10.clone.1 | loop fusion | flops 90242304 | bytes 21338880 | tf_op jit(solution)/shard_map/while/body/eval_jaxpr/reduce_sum | solution.py:76
  679.3 19.7 %fusion.61 = bf16[1,768,128]{2,1,0:T(8,128)(2,1)S(1)} fusion(bf16[6912,768]{1,0:T(8,128)(2,1)} %get-tuple-element.234, s32[]{:T(128)S(6)} %select_n.118, f32[768,6912]{1,0:T(8,128)S(1)} %get-tuple-element.193, f32[768]{0:T(1024)S(1)} %get-tuple-element.194, f32[768]{0:T(1024)S(1)} %fusion.60, s32[6912]{0:T(1024)S(1)} %get-tuple-element.239, ...), kind=kOutput, calls=%fused_computation.18.clone.1 | convolution fusion | flops 1449394176 | bytes 23304964 | tf_op jit(solution)/shard_map/while/body/eval_jaxpr/dot_general | solution.py:78
  702.5 18.2 %fusion.59 = (f32[768]{0:T(1024)S(1)}, f32[768,6912]{1,0:T(8,128)S(1)}) fusion(pred[6912]{0:T(1024)(128)(4,1)S(1)} %get-tuple-element.241, s32[6912]{0:T(1024)S(1)} %get-tuple-element.239, s32[768]{0:T(1024)S(1)} %get-tuple-element.240, s32[6912]{0:T(1024)S(1)} %get-tuple-element.237, s32[768]{0:T(1024)S(1)} %get-tuple-element.238, ...), kind=kOutput, calls=%fused_computation.9.clone.1 | convolution fusion | flops 1438579968 | bytes 23302912 | tf_op jit(solution)/shard_map/while/body/eval_jaxpr/dot_general | solution.py:70
  720.7 20.6 %fusion.60 = f32[768]{0:T(1024)S(1)} fusion(f32[768,6912]{1,0:T(8,128)S(1)} %get-tuple-element.193, f32[768]{0:T(1024)S(1)} %get-tuple-element.194, pred[6912]{0:T(1024)(128)(4,1)S(1)} %get-tuple-element.241, s32[6912]{0:T(1024)S(1)} %get-tuple-element.239, s32[768]{0:T(1024)S(1)} %get-tuple-element.240, s32[6912]{0:T(1024)S(1)} %get-tuple-element.237, ...), kind=kLoop, calls=%fused_computation.10.clone.1 | loop fusion | flops 90242304 | bytes 21338880 | tf_op jit(solution)/shard_map/while/body/eval_jaxpr/reduce_sum | solution.py:76
  741.3 19.4 %fusion.61 = bf16[1,768,128]{2,1,0:T(8,128)(2,1)S(1)} fusion(bf16[6912,768]{1,0:T(8,128)(2,1)} %get-tuple-element.234, s32[]{:T(128)S(6)} %select_n.118, f32[768,6912]{1,0:T(8,128)S(1)} %get-tuple-element.193, f32[768]{0:T(1024)S(1)} %get-tuple-element.194, f32[768]{0:T(1024)S(1)} %fusion.60, s32[6912]{0:T(1024)S(1)} %get-tuple-element.239, ...), kind=kOutput, calls=%fused_computation.18.clone.1 | convolution fusion | flops 1449394176 | bytes 23304964 | tf_op jit(solution)/shard_map/while/body/eval_jaxpr/dot_general | solution.py:78
  765.1 7.9 convolution_convert_fusion
  773.0 59.4 %reduce-scatter.2.cloned.1.call-done = bf16[768,768]{1,0:T(8,128)(2,1)} async-done(((bf16[768,3072]{1,0:T(8,128)(2,1)}), bf16[768,768]{1,0:T(8,128)(2,1)}) %reduce-scatter.2.cloned.1.call-update) | async-done | bytes 1179664 | tf_op jit(solution)/shard_map/reduce_scatter | solution.py:87
  (49 shorter events, 7.5 us)
Async XLA Ops:
  6.5 825.9 %reduce-scatter.2.cloned.1.call-start = ((), (), s32[]{:S(2)}) async-start(), calls=%async_computation.1 | async-start | bytes 5898240 | tf_op jit(solution)/shard_map/reduce_scatter | solution.py:87
  6.5 54.2 %collective-permute-start = (bf16[2,12,8,8,768]{4,3,2,1,0:T(8,128)(2,1)}, bf16[2,12,8,8,768]{4,3,2,1,0:T(8,128)(2,1)S(1)}, u32[]{:S(2)}, u32[]{:S(2)}) collective-permute-start(bf16[2,12,8,8,768]{4,3,2,1,0:T(8,128)(2,1)} %param.6), channel_id=1, source_target_pairs={{0,4},{4,8},{8,12},{1,5},{5,9},{9,13},{2,6},{6,10},{10,14},{3,7},{... | collective-permute-start | bytes 7077896 | tf_op jit(solution)/shard_map/ppermute | solution.py:20
  10.7 55.0 %collective-permute-start.1 = (bf16[2,12,8,8,768]{4,3,2,1,0:T(8,128)(2,1)}, bf16[2,12,8,8,768]{4,3,2,1,0:T(8,128)(2,1)S(1)}, u32[]{:S(2)}, u32[]{:S(2)}) collective-permute-start(bf16[2,12,8,8,768]{4,3,2,1,0:T(8,128)(2,1)} %param.6), channel_id=1, source_target_pairs={{4,0},{8,4},{12,8},{5,1},{9,5},{13,9},{6,2},{10,6},{14,10},{7,3},{... | collective-permute-start | bytes 7077896 | tf_op jit(solution)/shard_map/ppermute | solution.py:22
  67.3 153.5 %collective-permute-start.2 = (bf16[2,12,24,8,768]{4,3,2,1,0:T(8,128)(2,1)}, bf16[2,12,24,8,768]{4,3,2,1,0:T(8,128)(2,1)}, u32[]{:S(2)}, u32[]{:S(2)}) collective-permute-start(bf16[2,12,24,8,768]{4,3,2,1,0:T(8,128)(2,1)} %constant_dynamic-update-slice_fusion.1), channel_id=1, source_target_pairs={{0,16},{16,32},{32,48},{48,64},{64,80},{80,96},{96,112},{1,17},{17... | collective-permute-start | bytes 21233672 | tf_op jit(solution)/shard_map/ppermute | solution.py:20
  73.4 301.5 %collective-permute-start.3 = (bf16[2,12,24,8,768]{4,3,2,1,0:T(8,128)(2,1)}, bf16[2,12,24,8,768]{4,3,2,1,0:T(8,128)(2,1)}, u32[]{:S(2)}, u32[]{:S(2)}) collective-permute-start(bf16[2,12,24,8,768]{4,3,2,1,0:T(8,128)(2,1)} %constant_dynamic-update-slice_fusion.1), channel_id=1, source_target_pairs={{16,0},{32,16},{48,32},{64,48},{80,64},{96,80},{112,96},{17,1},{33... | collective-permute-start | bytes 21233672 | tf_op jit(solution)/shard_map/ppermute | solution.py:22
Sparse Core Ops, SparseCore 0:
  773.1 59.2 reduce-scatter.1
where the time goes:
time: 843 us; the launch traced here: 840 us
  waiting for transfers between devices  407 us (48%)
  matrix products  234 us (28%)
  other arithmetic  132 us (16%)
  local copies, waits for them, and re-layouts  20 us (2%)
  loops' own time  19 us (2%)
  between operations  13.9 us (2%)
  starting transfers between devices  12.8 us (2%)
    ppermute x2, waiting for transfers between devices, extended_2(): lax.ppermute(tail, axis, [(i, (i + 1) % count) for i in range(ends)])  194 us
    ppermute x2, waiting for transfers between devices, extended_2(): lax.ppermute(head, axis, [((i + 1) % count, i) for i in range(ends)])  154 us
    reduce_sum x6, other arithmetic, one_head(): row_total = jnp.sum(weights, axis=1, keepdims=True)  123 us
    dot_general x6, matrix products, one_head(): jnp.dot(weights.astype(jnp.bfloat16), head_values, preferred_element_type...  117 us
    dot_general x6, matrix products, one_head(): lax.dot_general(head_queries, head_keys, (((1,), (1,)), ((), ())), prefer...  109 us
    reduce_scatter x1, waiting for transfers between devices, body(): lax.psum_scatter(partial_rows.astype(jnp.bfloat16), 'ta', scatter_dimensi...  59.4 us
    another operation x1, loops' own time, body(): attended = lax.map(one_head, jnp.arange(heads_here, dtype=jnp.int32))  19 us
  transfers between devices with their start and end apart: 5, of which 4 were waited for; matrix products, arithmetic and copies ran while one was open for 1% of the time, Pallas kernels for 0%

commit v1 on v0

v1 whole, which is shorter than its diff:
```python
import functools

import jax
import jax.numpy as jnp
from jax import lax
from jax.experimental import pallas as pl
from jax.experimental.pallas import tpu as pltpu
from jax.sharding import PartitionSpec as P

HD = 128
LOG2E = 1.4426950408889634
EXP_SCALE = HD ** (-0.5) * LOG2E
BQ = 256
LOW = -1e30


def attend_kernel(gates, first, last, *refs):
    flags_ref, q_ref = refs[:2]
    tiles = refs[2 : 2 + len(gates)]
    rest = refs[2 + len(gates) :]
    if not first:
        acc_in, top_in = rest[:2]
        rest = rest[2:]
    tokens = q_ref.shape[0]
    span = tiles[0].shape[1]
    inside = [None if gate is None else flags_ref[gate] > 0 for gate in gates]

    def scores_of(start):
        queries = q_ref[pl.ds(start, BQ), :]
        return [
            lax.dot_general(
                queries, tile[0], (((1,), (1,)), ((), ())), preferred_element_type=jnp.float32
            )
            for tile in tiles
        ]

    def finish(start, scores):
        rows = pl.ds(start, BQ)
        old = jnp.full((BQ, HD), LOW, jnp.float32) if first else top_in[rows, :]
        new = old
        for score, valid in zip(scores, inside):
            largest = jnp.broadcast_to(jnp.max(score, axis=1, keepdims=True), (BQ, HD))
            if valid is not None:
                largest = jnp.where(valid, largest, LOW)
            new = jnp.maximum(new, largest)
        mixed = None
        for score, valid, tile in zip(scores, inside, tiles):
            shift = new if valid is None else jnp.where(valid, new, -LOW)
            wide = jnp.concatenate([shift] * (span // HD), axis=1)
            weights = jnp.exp2((score - wide) * EXP_SCALE).astype(jnp.bfloat16)
            values = jnp.concatenate([tile[1], jnp.ones((span, HD), jnp.bfloat16)], axis=1)
            part = jnp.dot(weights, values, preferred_element_type=jnp.float32)
            mixed = part if mixed is None else mixed + part
        if not first:
            keep = jnp.exp2((old - new) * EXP_SCALE)
            mixed = acc_in[rows, :] * jnp.concatenate([keep, keep], axis=1) + mixed
        if last:
            rest[0][rows, :] = (mixed[:, :HD] / mixed[:, HD:]).astype(rest[0].dtype)
        else:
            rest[0][rows, :] = mixed
            rest[1][rows, :] = new

    scores = scores_of(0)
    for start in range(0, tokens, BQ):
        following = scores_of(start + BQ) if start + BQ < tokens else None
        finish(start, scores)
        scores = following


def attend(flags, queries, tiles, gates, state=None, last=False):
    tokens, channels = queries.shape
    heads = channels // HD
    span = tiles[0].shape[1]
    q_spec = pl.BlockSpec((tokens, HD), lambda h: (0, h))
    acc_spec = pl.BlockSpec((tokens, 2 * HD), lambda h: (0, h))
    tile_spec = pl.BlockSpec((2, span, HD), lambda h: (0, 0, h))
    in_specs = [pl.BlockSpec(memory_space=pltpu.SMEM), q_spec] + [tile_spec] * len(tiles)
    args = [flags, queries, *tiles]
    if state is not None:
        in_specs += [acc_spec, q_spec]
        args += list(state)
    if last:
        out_shape = jax.ShapeDtypeStruct((tokens, channels), jnp.bfloat16)
        out_specs = q_spec
    else:
        out_shape = [
            jax.ShapeDtypeStruct((tokens, 2 * channels), jnp.float32),
            jax.ShapeDtypeStruct((tokens, channels), jnp.float32),
        ]
        out_specs = [acc_spec, q_spec]
    pairs = len(tiles) * heads * tokens * span
    return pl.pallas_call(
        functools.partial(attend_kernel, tuple(gates), state is None, last),
        out_shape=out_shape,
        grid=(heads,),
        in_specs=in_specs,
        out_specs=out_specs,
        compiler_params=pltpu.CompilerParams(vmem_limit_bytes=48 * 1024 * 1024),
        cost_estimate=pl.CostEstimate(
            flops=pairs * 8 * HD, bytes_accessed=len(tiles) * span * channels * 4, transcendentals=pairs
        ),
    )(*args)


def after(value, *others):
    return lax.optimization_barrier((value, *others))[0]


def body(queries, keys_values, out_weight):
    frames, rows, cols, channels = queries.shape
    tokens = frames * rows * cols
    half = channels // 2
    ha_count, wa_count = lax.axis_size("ha"), lax.axis_size("wa")
    ha, wa, ta = lax.axis_index("ha"), lax.axis_index("wa"), lax.axis_index("ta")
    odd = lax.rem(ha, 2)

    q_all = queries.reshape(tokens, channels)
    kv_all = keys_values.reshape(2, tokens, channels)
    keep_at, send_at = odd * half, (1 - odd) * half

    swap_pairs = [(i, i ^ 1) for i in range(ha_count)]
    native_pairs = [(i, (i + (2 if i % 2 else -2)) % ha_count) for i in range(ha_count)]
    swapped_pairs = [(i, (i + (-2 if i % 2 else 2)) % ha_count) for i in range(ha_count)]
    down_pairs = [(i, (i + 1) % wa_count) for i in range(wa_count)]
    up_pairs = [((i + 1) % wa_count, i) for i in range(wa_count)]

    def above_below(cells):
        return lax.ppermute(cells, "wa", down_pairs), lax.ppermute(cells, "wa", up_pairs)

    above, below = wa > 0, wa < wa_count - 1
    low, high = ha >= 2, ha < ha_count - 2
    far_partner = jnp.where(odd == 1, low, high)
    far_native = jnp.where(odd == 1, high, low)
    flags = jnp.stack(
        [above, below, far_partner, far_partner & above, far_partner & below,
         far_native, far_native & above, far_native & below]
    ).astype(jnp.int32)

    kv_send = lax.dynamic_slice_in_dim(kv_all, send_at, half, 2)
    kv_own = lax.dynamic_slice_in_dim(kv_all, keep_at, half, 2)
    q_send = lax.dynamic_slice_in_dim(q_all, send_at, half, 1)
    q_own = lax.dynamic_slice_in_dim(q_all, keep_at, half, 1)

    kv_pair = lax.ppermute(kv_send, "ha", swap_pairs)
    own_up, own_down = above_below(kv_own)
    far_p = lax.ppermute(kv_own, "ha", native_pairs)
    q_pair = lax.ppermute(after(q_send, kv_pair), "ha", swap_pairs)
    pair_up, pair_down = above_below(kv_pair)
    far_n = lax.ppermute(kv_pair, "ha", swapped_pairs)
    far_p_up = lax.ppermute(own_up, "ha", native_pairs)
    far_p_down = lax.ppermute(own_down, "ha", native_pairs)
    far_n_up, far_n_down = above_below(far_n)

    state_n = attend(flags, q_own, [kv_own], [None])
    state_n = attend(flags, q_own, [kv_pair, own_up, own_down], [None, 0, 1], state_n)
    state_p = attend(flags, q_pair, [kv_own, kv_pair, own_up, own_down, far_p], [None, None, 0, 1, 2])
    state_p = attend(flags, q_pair, [pair_up, pair_down], [0, 1], state_p)
    state_n = attend(flags, q_own, [pair_up, pair_down, far_n], [0, 1, 5], state_n)
    out_p = attend(flags, q_pair, [far_p_up, far_p_down], [3, 4], state_p, last=True)
    back = lax.ppermute(out_p, "ha", swap_pairs)
    out_n = attend(flags, q_own, [far_n_up, far_n_down], [6, 7], state_n, last=True)

    core, x_hi = lax.rem(ta, 2), ta // 2
    width = out_weight.shape[1] // lax.axis_size("ta")
    weight_n = lax.dynamic_slice_in_dim(out_weight, keep_at, half, 0)
    weight_p = lax.dynamic_slice_in_dim(out_weight, send_at, half, 0)
    attention = jnp.concatenate([out_n, back], axis=1)
    weight = jnp.concatenate([weight_n, weight_p], axis=0)

    def partial_of(group):
        columns = lax.dynamic_slice_in_dim(weight, group * width, width, 1)
        return jnp.dot(attention, columns, preferred_element_type=jnp.float32)

    core_pairs = [(i, i ^ 1) for i in range(4)]
    hi_pairs = [(i, i ^ 2) for i in range(4)]
    away_other = partial_of(2 * (1 - x_hi) + 1 - core).astype(jnp.bfloat16)
    away_in = lax.ppermute(away_other, "ta", core_pairs)
    away = (partial_of(2 * (1 - x_hi) + core) + away_in.astype(jnp.float32)).astype(jnp.bfloat16)
    home_far = lax.ppermute(away, "ta", hi_pairs)
    home_other = partial_of(2 * x_hi + 1 - core).astype(jnp.bfloat16)
    home_in = lax.ppermute(home_other, "ta", core_pairs)
    home = partial_of(ta) + home_in.astype(jnp.float32) + home_far.astype(jnp.float32)
    return home.astype(jnp.bfloat16).reshape(frames, rows, cols, width)


def solution(mesh):
    return jax.shard_map(
        body,
        mesh=mesh,
        in_specs=(P(None, "wa", "ha", "ta"), P(None, None, "wa", "ha", "ta"), P("ta", None)),
        out_specs=P(None, "wa", "ha", "ta"),
        check_vma=False,
    )
```

time: 843 us -> 177 us (0.21)
  waiting for transfers between devices: 407 us -> 60.3 us
  matrix products: 234 us -> 11 us
  other arithmetic: 132 us -> 3.08 us
  Pallas kernels: 0 us -> 59.1 us
  loops' own time: 19 us -> 0 us
  starting transfers between devices: 12.8 us -> 30.7 us
  between operations: 13.9 us -> 0.14 us
    ppermute x4 -> x16, waiting for transfers between devices: 348 us -> 60.3 us  [the longest x1 24 us: body(): home_far = lax.ppermute(away, 'ta', hi_pairs)]
    dot_general x13 -> x4, matrix products: 234 us -> 11 us  [partial_of(): return jnp.dot(attention, columns, preferred_element_type=jnp.float32)]
    reduce_sum x6 -> x0, other arithmetic: 123 us -> none  [one_head(): row_total = jnp.sum(weights, axis=1, keepdims=True)]
    reduce_scatter x1 -> x0, waiting for transfers between devices: 59.4 us -> none  [body(): lax.psum_scatter(partial_rows.astype(jnp.bfloat16), 'ta', scatter_dimensi...]
    pallas_call x0 -> x7, Pallas kernels: none -> 59.1 us  [attend(): pl.pallas_call(functools.partial(attend_kernel, tuple(gates), state is No...]
    another operation x1 -> x0, loops' own time: 19 us -> none  [body(): attended = lax.map(one_head, jnp.arange(heads_here, dtype=jnp.int32))]
    ppermute x4 -> x16, starting transfers between devices: 12.8 us -> 30.7 us  [the longest x3 5.61 us: above_below(): lax.ppermute(cells, 'wa', up_pairs)]
    concatenate x1 -> x0, other arithmetic: 9.59 us -> none  [extended_2(): jnp.concatenate([lax.ppermute(tail, axis, [(i, (i + 1) % count) for i in...]
  transfers between devices with their start and end apart: 5 -> 16, of which waited for: 4 -> 3; matrix products, arithmetic and copies ran while one was open for 1% -> 8% of each run, Pallas kernels for 0% -> 33%
where the time goes in v1:
time: 177 us
  waiting for transfers between devices  60.3 us (34%)
  Pallas kernels  59.1 us (33%)
  starting transfers between devices  30.7 us (17%)
  local copies, waits for them, and re-layouts  12.4 us (7%)
  matrix products  11 us (6%)
  other arithmetic  3.08 us (2%)
    pallas_call x7, Pallas kernels, attend(): pl.pallas_call(functools.partial(attend_kernel, tuple(gates), state is No...  59.1 us
    ppermute x1, waiting for transfers between devices, body(): home_far = lax.ppermute(away, 'ta', hi_pairs)  24 us
    ppermute x1, waiting for transfers between devices, body(): far_p_up = lax.ppermute(own_up, 'ha', native_pairs)  23.2 us
    ppermute x1, waiting for transfers between devices, body(): kv_pair = lax.ppermute(kv_send, 'ha', swap_pairs)  13.1 us
    dot_general x4, matrix products, partial_of(): return jnp.dot(attention, columns, preferred_element_type=jnp.float32)  11 us
    ppermute x3, starting transfers between devices, above_below(): lax.ppermute(cells, 'wa', up_pairs)  5.61 us
    dynamic_slice x1, local copies, waits for them, and re-layouts, body(): weight_p = lax.dynamic_slice_in_dim(out_weight, send_at, half, 0)  4.85 us
    ppermute x1, starting transfers between devices, body(): far_p = lax.ppermute(kv_own, 'ha', native_pairs)  3.76 us
  transfers between devices with their start and end apart: 16, of which 3 were waited for; matrix products, arithmetic and copies ran while one was open for 8% of the time, Pallas kernels for 33%

profile of v1, /device:TPU:1, one launch (start us, length us, event | category | flops | bytes accessed | tf_op | source)
XLA Modules:
  0.0 176.7 jit_solution(5105915639362117066)
XLA Ops:
  0.0 3.0 %constant_dynamic-slice_fusion.3 = (bf16[2,768,384]{2,1,0:T(8,128)(2,1)S(1)}, bf16[2,768,384]{2,1,0:T(8,128)(2,1)}) fusion(bf16[2,768,768]{2,1,0:T(8,128)(2,1)} %bitcast.11, s32[]{:T(128)S(6)} %select_n.36, s32[]{:T(128)S(6)} %select_n.37), kind=kLoop, calls=%fused_computation.25 | loop fusion | bytes 4718600 | tf_op jit(solution)/shard_map/dynamic_slice | solution.py:140
  3.0 2.0 %collective-permute-start = (bf16[2,768,384]{2,1,0:T(8,128)(2,1)}, bf16[2,768,384]{2,1,0:T(8,128)(2,1)}, u32[]{:S(2)}, u32[]{:S(2)}) collective-permute-start(bf16[2,768,384]{2,1,0:T(8,128)(2,1)} %get-tuple-element.30), channel_id=1, source_target_pairs={{0,16},{16,0},{32,48},{48,32},{64,80},{80,64},{96,112},{112,96},{1... | collective-permute-start | bytes 3538952 | tf_op jit(solution)/shard_map/ppermute | solution.py:144
  5.0 1.3 collective-permute-start.6
  6.3 1.4 collective-permute-start.7
  7.8 3.8 %collective-permute-start.11 = (bf16[2,768,384]{2,1,0:T(8,128)(2,1)S(1)}, bf16[2,768,384]{2,1,0:T(8,128)(2,1)}, u32[]{:S(2)}, u32[]{:S(2)}) collective-permute-start(bf16[2,768,384]{2,1,0:T(8,128)(2,1)S(1)} %get-tuple-element.29.refs_2_), channel_id=1, source_target_pairs={{0,96},{16,48},{32,0},{48,80},{64,32},{80,112},{96,64},{112,16},{1... | collective-permute-start | bytes 3538952 | tf_op jit(solution)/shard_map/ppermute | solution.py:146
  12.6 4.8 %constant_dynamic-slice_fusion = (bf16[384,3072]{1,0:T(8,128)(2,1)}, bf16[384,3072]{1,0:T(8,128)(2,1)}) fusion(bf16[768,3072]{1,0:T(8,128)(2,1)} %param.5, s32[]{:T(128)S(6)} %select_n.37, s32[]{:T(128)S(6)} %select_n.36), kind=kLoop, calls=%fused_computation.22 | loop fusion | bytes 9437192 | tf_op jit(solution)/shard_map/dynamic_slice | solution.py:166
  17.4 13.1 %collective-permute-done.refs_2_.refs_3_ = bf16[2,768,384]{2,1,0:T(8,128)(2,1)} collective-permute-done((bf16[2,768,384]{2,1,0:T(8,128)(2,1)}, bf16[2,768,384]{2,1,0:T(8,128)(2,1)}, u32[]{:S(2)}, u32[]{:S(2)}) %collective-permute-start) | collective-permute-done | bytes 1179680 | tf_op jit(solution)/shard_map/ppermute | solution.py:144
  30.5 1.7 collective-permute-start.8
  32.2 4.1 %shard_map.37 = (f32[768,768]{1,0:T(8,128)S(1)}, f32[768,384]{1,0:T(8,128)S(1)}) custom-call(s32[8]{0:T(128)S(1)} %convert_element_type.24.refs_0_, bf16[768,384]{1,0:T(8,128)(2,1)S(1)} %get-tuple-element.31.refs_1_, bf16[2,768,384]{2,1,0:T(8,128)(2,1)S(1)} %get-tuple-element.29.refs_2_), custom_call_target="tpu_custom_call" | custom-call | flops 1811939328 | bytes 1179648 | tf_op jit(solution)/shard_map/pallas_call | solution.py:92
  36.3 1.5 copy-done
  38.8 1.6 collective-permute-start.1
  40.4 1.3 collective-permute-start.4
  41.7 1.5 collective-permute-start.5
  43.2 9.7 %shard_map.38 = (f32[768,768]{1,0:T(8,128)}, f32[768,384]{1,0:T(8,128)S(1)}) custom-call(s32[8]{0:T(128)S(1)} %convert_element_type.24.refs_0_, bf16[768,384]{1,0:T(8,128)(2,1)S(1)} %get-tuple-element.31.refs_1_, bf16[2,768,384]{2,1,0:T(8,128)(2,1)} %collective-permute-done.refs_2_.refs_3_, bf16[2,768,384]{2,1,0:T(8,128)(2,1)S(1)} %collective-permute-done.6.refs_3_.refs_4_, ...), custom_call_target="tpu_custom_call" | custom-call | flops 5435817984 | bytes 3538944 | tf_op jit(solution)/shard_map/pallas_call | solution.py:92
  53.9 2.1 %collective-permute-start.10 = (bf16[2,768,384]{2,1,0:T(8,128)(2,1)}, bf16[2,768,384]{2,1,0:T(8,128)(2,1)S(1)}, u32[]{:S(2)}, u32[]{:S(2)}) collective-permute-start(bf16[2,768,384]{2,1,0:T(8,128)(2,1)} %collective-permute-done.7.refs_4_.refs_5_), channel_id=1, source_target_pairs={{0,96},{16,48},{32,0},{48,80},{64,32},{80,112},{96,64},{112,16},{1... | collective-permute-start | bytes 3538952 | tf_op jit(solution)/shard_map/ppermute | solution.py:151
  56.0 1.5 collective-permute-start.9
  57.5 13.5 %shard_map.41 = (f32[768,768]{1,0:T(8,128)}, f32[768,384]{1,0:T(8,128)S(1)}) custom-call(s32[8]{0:T(128)S(1)} %convert_element_type.24.refs_0_, bf16[768,384]{1,0:T(8,128)(2,1)S(1)} %collective-permute-done.8.refs_1_, bf16[2,768,384]{2,1,0:T(8,128)(2,1)S(1)} %get-tuple-element.29.refs_2_, bf16[2,768,384]{2,1,0:T(8,128)(2,1)} %collective-permute-done.refs_2_.refs_3_, ...), custom_call_target="tpu_custom_call" | custom-call | flops 9059696640 | bytes 5898240 | tf_op jit(solution)/shard_map/pallas_call | solution.py:92
  71.0 2.7 %collective-permute-start.3 = (bf16[2,768,384]{2,1,0:T(8,128)(2,1)S(1)}, bf16[2,768,384]{2,1,0:T(8,128)(2,1)S(1)}, u32[]{:S(2)}, u32[]{:S(2)}) collective-permute-start(bf16[2,768,384]{2,1,0:T(8,128)(2,1)S(1)} %collective-permute-done.1.refs_4_), channel_id=1, source_target_pairs={{4,0},{8,4},{12,8},{0,12},{5,1},{9,5},{13,9},{1,13},{6,2},{10,6},{... | collective-permute-start | bytes 3538952 | tf_op jit(solution)/shard_map/ppermute | solution.py:128
  73.7 7.7 %shard_map.42 = (f32[768,768]{1,0:T(8,128)}, f32[768,384]{1,0:T(8,128)S(1)}) custom-call(s32[8]{0:T(128)S(1)} %convert_element_type.24.refs_0_, bf16[768,384]{1,0:T(8,128)(2,1)S(1)} %collective-permute-done.8.refs_1_, bf16[2,768,384]{2,1,0:T(8,128)(2,1)S(1)} %collective-permute-done.4.refs_2_, bf16[2,768,384]{2,1,0:T(8,128)(2,1)S(1)} %collective-permute-done.5.refs_3_, ...), custom_call_target="tpu_custom_call" | custom-call | flops 3623878656 | bytes 2359296 | tf_op jit(solution)/shard_map/pallas_call | solution.py:92
  81.4 23.2 %collective-permute-done.9.refs_2_ = bf16[2,768,384]{2,1,0:T(8,128)(2,1)S(1)} collective-permute-done((bf16[2,768,384]{2,1,0:T(8,128)(2,1)S(1)}, bf16[2,768,384]{2,1,0:T(8,128)(2,1)S(1)}, u32[]{:S(2)}, u32[]{:S(2)}) %collective-permute-start.9) | collective-permute-done | bytes 1179680 | tf_op jit(solution)/shard_map/ppermute | solution.py:150
  104.7 6.9 %shard_map.43 = bf16[768,384]{1,0:T(8,128)(2,1)S(1)} custom-call(s32[8]{0:T(128)S(1)} %convert_element_type.24.refs_0_, bf16[768,384]{1,0:T(8,128)(2,1)S(1)} %collective-permute-done.8.refs_1_, bf16[2,768,384]{2,1,0:T(8,128)(2,1)S(1)} %collective-permute-done.9.refs_2_, bf16[2,768,384]{2,1,0:T(8,128)(2,1)S(1)} %collective-permute-done.10.refs_3_, ...), custom_call_target="tpu_custom_call" | custom-call | flops 3623878656 | bytes 2359296 | tf_op jit(solution)/shard_map/pallas_call | solution.py:92
  111.6 3.3 %collective-permute-start.12 = (bf16[768,384]{1,0:T(8,128)(2,1)S(1)}, bf16[768,384]{1,0:T(8,128)(2,1)S(1)}, u32[]{:S(2)}, u32[]{:S(2)}) collective-permute-start(bf16[768,384]{1,0:T(8,128)(2,1)S(1)} %shard_map.43), channel_id=1, source_target_pairs={{0,16},{16,0},{32,48},{48,32},{64,80},{80,64},{96,112},{112,96},{1... | collective-permute-start | bytes 1769480 | tf_op jit(solution)/shard_map/ppermute | solution.py:160
  114.9 10.1 %shard_map.39 = (f32[768,768]{1,0:T(8,128)}, f32[768,384]{1,0:T(8,128)S(1)}) custom-call(s32[8]{0:T(128)S(1)} %convert_element_type.24.refs_0_, bf16[768,384]{1,0:T(8,128)(2,1)S(1)} %get-tuple-element.31.refs_1_, bf16[2,768,384]{2,1,0:T(8,128)(2,1)S(1)} %collective-permute-done.4.refs_2_, bf16[2,768,384]{2,1,0:T(8,128)(2,1)S(1)} %collective-permute-done.5.refs_3_, ...), custom_call_target="tpu_custom_call" | custom-call | flops 5435817984 | bytes 3538944 | tf_op jit(solution)/shard_map/pallas_call | solution.py:92
  125.0 7.1 %shard_map.40 = bf16[768,384]{1,0:T(8,128)(2,1)S(1)} custom-call(s32[8]{0:T(128)S(1)} %convert_element_type.24.refs_0_, bf16[768,384]{1,0:T(8,128)(2,1)S(1)} %get-tuple-element.31.refs_1_, bf16[2,768,384]{2,1,0:T(8,128)(2,1)S(1)} %collective-permute-done.2.refs_2_, bf16[2,768,384]{2,1,0:T(8,128)(2,1)S(1)} %collective-permute-done.3.refs_3_, ...), custom_call_target="tpu_custom_call" | custom-call | flops 3623878656 | bytes 2359296 | tf_op jit(solution)/shard_map/pallas_call | solution.py:92
  132.1 2.1 %convolution_convert_fusion = bf16[768,768]{1,0:T(8,128)(2,1)} fusion(s32[]{:T(128)S(6)} %select_n.42, bf16[384,3072]{1,0:T(8,128)(2,1)S(1)} %copy-done.5, bf16[384,3072]{1,0:T(8,128)(2,1)S(1)} %copy-done.3, bf16[768,384]{1,0:T(8,128)(2,1)S(1)} %collective-permute-done.12, bf16[768,384]{1,0:T(8,128)(2,1)S(1)} %shard_map.40), kind=kOutput, calls=%fused_computation.10 | convolution fusion | flops 911278080 | bytes 7077892 | tf_op jit(solution)/shard_map/dot_general | solution.py:172
  134.3 3.8 %collective-permute-start.14 = (bf16[768,768]{1,0:T(8,128)(2,1)}, bf16[768,768]{1,0:T(8,128)(2,1)}, u32[]{:S(2)}, u32[]{:S(2)}) collective-permute-start(bf16[768,768]{1,0:T(8,128)(2,1)} %convolution_convert_fusion), channel_id=1, source_target_pairs={{0,1},{1,0},{2,3},{3,2},{4,5},{5,4},{6,7},{7,6},{8,9},{9,8},{10,11... | collective-permute-start | bytes 3538952 | tf_op jit(solution)/shard_map/ppermute | solution.py:177
  138.0 3.3 %convolution_convert_fusion.1 = bf16[768,768]{1,0:T(8,128)(2,1)} fusion(s32[]{:T(128)S(6)} %select_n.40, bf16[384,3072]{1,0:T(8,128)(2,1)} %get-tuple-element.28, bf16[384,3072]{1,0:T(8,128)(2,1)S(1)} %copy-done.4, bf16[768,384]{1,0:T(8,128)(2,1)S(1)} %collective-permute-done.12, bf16[768,384]{1,0:T(8,128)(2,1)S(1)} %shard_map.40), kind=kOutput, calls=%fused_computation.11 | convolution fusion | flops 911278080 | bytes 7077892 | tf_op jit(solution)/shard_map/dot_general | solution.py:172
  141.4 3.4 %add_convert_fusion.1 = bf16[768,768]{1,0:T(8,128)(2,1)} fusion(bf16[768,768]{1,0:T(8,128)(2,1)} %collective-permute-done.14, s32[]{:T(128)S(6)} %select_n.41, bf16[384,3072]{1,0:T(8,128)(2,1)S(1)} %copy-done.6, bf16[384,3072]{1,0:T(8,128)(2,1)S(1)} %copy-done.4, bf16[768,384]{1,0:T(8,128)(2,1)S(1)} %collective-permute-done.12, ...), kind=kOutput, calls=%fused_computation.9 | convolution fusion | flops 912457728 | bytes 8257540 | tf_op jit(solution)/shard_map/dot_general | solution.py:172
  144.8 2.7 %collective-permute-start.15 = (bf16[768,768]{1,0:T(8,128)(2,1)}, bf16[768,768]{1,0:T(8,128)(2,1)}, u32[]{:S(2)}, u32[]{:S(2)}) collective-permute-start(bf16[768,768]{1,0:T(8,128)(2,1)} %add_convert_fusion.1), channel_id=1, source_target_pairs={{0,2},{1,3},{2,0},{3,1},{4,6},{5,7},{6,4},{7,5},{8,10},{9,11},{10,... | collective-permute-start | bytes 3538952 | tf_op jit(solution)/shard_map/ppermute | solution.py:179
  147.5 2.2 %fusion.3 = f32[768,768]{1,0:T(8,128)S(1)} fusion(s32[]{:T(128)S(6)} %select_n.38, bf16[384,3072]{1,0:T(8,128)(2,1)} %get-tuple-element.28, bf16[384,3072]{1,0:T(8,128)(2,1)S(1)} %copy-done.4, bf16[768,384]{1,0:T(8,128)(2,1)S(1)} %collective-permute-done.12, bf16[768,384]{1,0:T(8,128)(2,1)S(1)} %shard_map.40), kind=kOutput, calls=%fused_computation.14 | convolution fusion | flops 910688256 | bytes 8257540 | tf_op jit(solution)/shard_map/dot_general | solution.py:172
  149.7 24.0 %collective-permute-done.15 = bf16[768,768]{1,0:T(8,128)(2,1)} collective-permute-done((bf16[768,768]{1,0:T(8,128)(2,1)}, bf16[768,768]{1,0:T(8,128)(2,1)}, u32[]{:S(2)}, u32[]{:S(2)}) %collective-permute-start.15) | collective-permute-done | bytes 1179680 | tf_op jit(solution)/shard_map/ppermute | solution.py:179
  173.7 3.1 %add_convert_fusion = bf16[768,768]{1,0:T(8,128)(2,1)} fusion(bf16[768,768]{1,0:T(8,128)(2,1)} %collective-permute-done.15, f32[768,768]{1,0:T(8,128)S(1)} %fusion.3, bf16[768,768]{1,0:T(8,128)(2,1)} %collective-permute-done.13), kind=kLoop, calls=%fused_computation.8 | loop fusion | flops 2949120 | bytes 5898240 | tf_op jit(solution)/shard_map/convert_element_type | solution.py:183
  (33 shorter events, 3.2 us)
Async XLA Ops:
  0.0 11.5 %copy-start.7 = (bf16[12,8,8,768]{3,2,1,0:T(8,128)(2,1)S(1)}, bf16[12,8,8,768]{3,2,1,0:T(8,128)(2,1)}, u32[]{:S(2)}) copy-start(bf16[12,8,8,768]{3,2,1,0:T(8,128)(2,1)} %param.3) | copy-start | bytes 3538948
  3.0 27.5 %collective-permute-start = (bf16[2,768,384]{2,1,0:T(8,128)(2,1)}, bf16[2,768,384]{2,1,0:T(8,128)(2,1)}, u32[]{:S(2)}, u32[]{:S(2)}) collective-permute-start(bf16[2,768,384]{2,1,0:T(8,128)(2,1)} %get-tuple-element.30), channel_id=1, source_target_pairs={{0,16},{16,0},{32,48},{48,32},{64,80},{80,64},{96,112},{112,96},{1... | collective-permute-start | bytes 3538952 | tf_op jit(solution)/shard_map/ppermute | solution.py:144
  5.0 35.4 %collective-permute-start.6 = (bf16[2,768,384]{2,1,0:T(8,128)(2,1)S(1)}, bf16[2,768,384]{2,1,0:T(8,128)(2,1)S(1)}, u32[]{:S(2)}, u32[]{:S(2)}) collective-permute-start(bf16[2,768,384]{2,1,0:T(8,128)(2,1)S(1)} %get-tuple-element.29.refs_2_), channel_id=1, source_target_pairs={{0,4},{4,8},{8,12},{12,0},{1,5},{5,9},{9,13},{13,1},{2,6},{6,10},{... | collective-permute-start | bytes 3538952 | tf_op jit(solution)/shard_map/ppermute | solution.py:128
  6.3 35.4 %collective-permute-start.7 = (bf16[2,768,384]{2,1,0:T(8,128)(2,1)S(1)}, bf16[2,768,384]{2,1,0:T(8,128)(2,1)}, u32[]{:S(2)}, u32[]{:S(2)}) collective-permute-start(bf16[2,768,384]{2,1,0:T(8,128)(2,1)S(1)} %get-tuple-element.29.refs_2_), channel_id=1, source_target_pairs={{4,0},{8,4},{12,8},{0,12},{5,1},{9,5},{13,9},{1,13},{6,2},{10,6},{... | collective-permute-start | bytes 3538952 | tf_op jit(solution)/shard_map/ppermute | solution.py:128
  7.8 46.2 %collective-permute-start.11 = (bf16[2,768,384]{2,1,0:T(8,128)(2,1)S(1)}, bf16[2,768,384]{2,1,0:T(8,128)(2,1)}, u32[]{:S(2)}, u32[]{:S(2)}) collective-permute-start(bf16[2,768,384]{2,1,0:T(8,128)(2,1)S(1)} %get-tuple-element.29.refs_2_), channel_id=1, source_target_pairs={{0,96},{16,48},{32,0},{48,80},{64,32},{80,112},{96,64},{112,16},{1... | collective-permute-start | bytes 3538952 | tf_op jit(solution)/shard_map/ppermute | solution.py:146
  30.5 25.5 %collective-permute-start.8 = (bf16[768,384]{1,0:T(8,128)(2,1)}, bf16[768,384]{1,0:T(8,128)(2,1)S(1)}, u32[]{:S(2)}, u32[]{:S(2)}) collective-permute-start(bf16[768,384]{1,0:T(8,128)(2,1)} %get-tuple-element.22), channel_id=1, source_target_pairs={{0,16},{16,0},{32,48},{48,32},{64,80},{80,64},{96,112},{112,96},{1... | collective-permute-start | bytes 1769480 | tf_op jit(solution)/shard_map/ppermute | solution.py:147
  36.3 1.5 copy-start
  37.8 1.0 copy-start.1
  38.8 32.2 %collective-permute-start.1 = (bf16[2,768,384]{2,1,0:T(8,128)(2,1)}, bf16[2,768,384]{2,1,0:T(8,128)(2,1)S(1)}, u32[]{:S(2)}, u32[]{:S(2)}) collective-permute-start(bf16[2,768,384]{2,1,0:T(8,128)(2,1)} %collective-permute-done.refs_2_.refs_3_), channel_id=1, source_target_pairs={{0,32},{16,112},{32,64},{48,16},{64,96},{80,48},{96,0},{112,80},{1... | collective-permute-start | bytes 3538952 | tf_op jit(solution)/shard_map/ppermute | solution.py:149
  40.4 30.6 %collective-permute-start.4 = (bf16[2,768,384]{2,1,0:T(8,128)(2,1)}, bf16[2,768,384]{2,1,0:T(8,128)(2,1)S(1)}, u32[]{:S(2)}, u32[]{:S(2)}) collective-permute-start(bf16[2,768,384]{2,1,0:T(8,128)(2,1)} %collective-permute-done.refs_2_.refs_3_), channel_id=1, source_target_pairs={{0,4},{4,8},{8,12},{12,0},{1,5},{5,9},{9,13},{13,1},{2,6},{6,10},{... | collective-permute-start | bytes 3538952 | tf_op jit(solution)/shard_map/ppermute | solution.py:128
  41.7 32.0 %collective-permute-start.5 = (bf16[2,768,384]{2,1,0:T(8,128)(2,1)}, bf16[2,768,384]{2,1,0:T(8,128)(2,1)S(1)}, u32[]{:S(2)}, u32[]{:S(2)}) collective-permute-start(bf16[2,768,384]{2,1,0:T(8,128)(2,1)} %collective-permute-done.refs_2_.refs_3_), channel_id=1, source_target_pairs={{4,0},{8,4},{12,8},{0,12},{5,1},{9,5},{13,9},{1,13},{6,2},{10,6},{... | collective-permute-start | bytes 3538952 | tf_op jit(solution)/shard_map/ppermute | solution.py:128
  52.9 1.0 copy-start.2
  53.9 27.5 %collective-permute-start.10 = (bf16[2,768,384]{2,1,0:T(8,128)(2,1)}, bf16[2,768,384]{2,1,0:T(8,128)(2,1)S(1)}, u32[]{:S(2)}, u32[]{:S(2)}) collective-permute-start(bf16[2,768,384]{2,1,0:T(8,128)(2,1)} %collective-permute-done.7.refs_4_.refs_5_), channel_id=1, source_target_pairs={{0,96},{16,48},{32,0},{48,80},{64,32},{80,112},{96,64},{112,16},{1... | collective-permute-start | bytes 3538952 | tf_op jit(solution)/shard_map/ppermute | solution.py:151
  56.0 48.6 %collective-permute-start.9 = (bf16[2,768,384]{2,1,0:T(8,128)(2,1)S(1)}, bf16[2,768,384]{2,1,0:T(8,128)(2,1)S(1)}, u32[]{:S(2)}, u32[]{:S(2)}) collective-permute-start(bf16[2,768,384]{2,1,0:T(8,128)(2,1)S(1)} %collective-permute-done.6.refs_3_.refs_4_), channel_id=1, source_target_pairs={{0,96},{16,48},{32,0},{48,80},{64,32},{80,112},{96,64},{112,16},{1... | collective-permute-start | bytes 3538952 | tf_op jit(solution)/shard_map/ppermute | solution.py:150
  71.0 54.0 %collective-permute-start.2 = (bf16[2,768,384]{2,1,0:T(8,128)(2,1)S(1)}, bf16[2,768,384]{2,1,0:T(8,128)(2,1)S(1)}, u32[]{:S(2)}, u32[]{:S(2)}) collective-permute-start(bf16[2,768,384]{2,1,0:T(8,128)(2,1)S(1)} %collective-permute-done.1.refs_4_), channel_id=1, source_target_pairs={{0,4},{4,8},{8,12},{12,0},{1,5},{5,9},{9,13},{13,1},{2,6},{6,10},{... | collective-permute-start | bytes 3538952 | tf_op jit(solution)/shard_map/ppermute | solution.py:128
  71.0 54.0 %collective-permute-start.3 = (bf16[2,768,384]{2,1,0:T(8,128)(2,1)S(1)}, bf16[2,768,384]{2,1,0:T(8,128)(2,1)S(1)}, u32[]{:S(2)}, u32[]{:S(2)}) collective-permute-start(bf16[2,768,384]{2,1,0:T(8,128)(2,1)S(1)} %collective-permute-done.1.refs_4_), channel_id=1, source_target_pairs={{4,0},{8,4},{12,8},{0,12},{5,1},{9,5},{13,9},{1,13},{6,2},{10,6},{... | collective-permute-start | bytes 3538952 | tf_op jit(solution)/shard_map/ppermute | solution.py:128
  111.6 20.5 %collective-permute-start.12 = (bf16[768,384]{1,0:T(8,128)(2,1)S(1)}, bf16[768,384]{1,0:T(8,128)(2,1)S(1)}, u32[]{:S(2)}, u32[]{:S(2)}) collective-permute-start(bf16[768,384]{1,0:T(8,128)(2,1)S(1)} %shard_map.43), channel_id=1, source_target_pairs={{0,16},{16,0},{32,48},{48,32},{64,80},{80,64},{96,112},{112,96},{1... | collective-permute-start | bytes 1769480 | tf_op jit(solution)/shard_map/ppermute | solution.py:160
  125.0 7.1 %copy-start.3 = (bf16[384,3072]{1,0:T(8,128)(2,1)S(1)}, bf16[384,3072]{1,0:T(8,128)(2,1)}, u32[]{:S(2)}) copy-start(bf16[384,3072]{1,0:T(8,128)(2,1)} %get-tuple-element.27) | copy-start | bytes 7077892
  125.0 7.1 %copy-start.5 = (bf16[384,3072]{1,0:T(8,128)(2,1)S(1)}, bf16[384,3072]{1,0:T(8,128)(2,1)}, u32[]{:S(2)}) copy-start(bf16[384,3072]{1,0:T(8,128)(2,1)} %get-tuple-element.28) | copy-start | bytes 7077892
  132.1 5.9 %copy-start.4 = (bf16[384,3072]{1,0:T(8,128)(2,1)S(1)}, bf16[384,3072]{1,0:T(8,128)(2,1)}, u32[]{:S(2)}) copy-start(bf16[384,3072]{1,0:T(8,128)(2,1)} %get-tuple-element.27) | copy-start | bytes 7077892
  134.3 7.1 %collective-permute-start.14 = (bf16[768,768]{1,0:T(8,128)(2,1)}, bf16[768,768]{1,0:T(8,128)(2,1)}, u32[]{:S(2)}, u32[]{:S(2)}) collective-permute-start(bf16[768,768]{1,0:T(8,128)(2,1)} %convolution_convert_fusion), channel_id=1, source_target_pairs={{0,1},{1,0},{2,3},{3,2},{4,5},{5,4},{6,7},{7,6},{8,9},{9,8},{10,11... | collective-permute-start | bytes 3538952 | tf_op jit(solution)/shard_map/ppermute | solution.py:177
  138.0 3.3 %copy-start.6 = (bf16[384,3072]{1,0:T(8,128)(2,1)S(1)}, bf16[384,3072]{1,0:T(8,128)(2,1)}, u32[]{:S(2)}) copy-start(bf16[384,3072]{1,0:T(8,128)(2,1)} %get-tuple-element.28) | copy-start | bytes 7077892
  141.3 8.3 %collective-permute-start.13 = (bf16[768,768]{1,0:T(8,128)(2,1)}, bf16[768,768]{1,0:T(8,128)(2,1)}, u32[]{:S(2)}, u32[]{:S(2)}) collective-permute-start(bf16[768,768]{1,0:T(8,128)(2,1)} %convolution_convert_fusion.1), channel_id=1, source_target_pairs={{0,1},{1,0},{2,3},{3,2},{4,5},{5,4},{6,7},{7,6},{8,9},{9,8},{10,11... | collective-permute-start | bytes 3538952 | tf_op jit(solution)/shard_map/ppermute | solution.py:181
  144.8 28.9 %collective-permute-start.15 = (bf16[768,768]{1,0:T(8,128)(2,1)}, bf16[768,768]{1,0:T(8,128)(2,1)}, u32[]{:S(2)}, u32[]{:S(2)}) collective-permute-start(bf16[768,768]{1,0:T(8,128)(2,1)} %add_convert_fusion.1), channel_id=1, source_target_pairs={{0,2},{1,3},{2,0},{3,1},{4,6},{5,7},{6,4},{7,5},{8,10},{9,11},{10,... | collective-permute-start | bytes 3538952 | tf_op jit(solution)/shard_map/ppermute | solution.py:179

commit v2 on v1

v2 whole, which is shorter than its diff:
```python
import functools

import jax
import jax.numpy as jnp
from jax import lax
from jax.experimental import pallas as pl
from jax.experimental.pallas import tpu as pltpu
from jax.sharding import PartitionSpec as P

HD = 128
LOG2E = 1.4426950408889634
EXP_SCALE = HD ** (-0.5) * LOG2E
LOW = -1e30


COST2 = 1024


def attend_kernel(gates, first, last, step, *refs):
    flags_ref, q_ref = refs[:2]
    tiles = refs[2 : 2 + len(gates)]
    rest = refs[2 + len(gates) :]
    if not first:
        acc_in, top_in = rest[:2]
        rest = rest[2:]
    tokens = q_ref.shape[0]
    span = tiles[0].shape[1]
    inside = [None if gate is None else flags_ref[gate] > 0 for gate in gates]

    def scores_of(start):
        queries = q_ref[pl.ds(start, step), :]
        return [
            lax.dot_general(
                queries, tile[0], (((1,), (1,)), ((), ())), preferred_element_type=jnp.float32
            )
            for tile in tiles
        ]

    def finish(start, scores):
        rows = pl.ds(start, step)
        old = jnp.full((step, HD), LOW, jnp.float32) if first else top_in[rows, :]
        new = old
        for score, valid in zip(scores, inside):
            largest = jnp.broadcast_to(jnp.max(score, axis=1, keepdims=True), (step, HD))
            if valid is not None:
                largest = jnp.where(valid, largest, LOW)
            new = jnp.maximum(new, largest)
        mixed = None
        for score, valid, tile in zip(scores, inside, tiles):
            shift = new if valid is None else jnp.where(valid, new, -LOW)
            wide = jnp.concatenate([shift] * (span // HD), axis=1)
            weights = jnp.exp2((score - wide) * EXP_SCALE).astype(jnp.bfloat16)
            values = jnp.concatenate([tile[1], jnp.ones((span, HD), jnp.bfloat16)], axis=1)
            part = jnp.dot(weights, values, preferred_element_type=jnp.float32)
            mixed = part if mixed is None else mixed + part
        if not first:
            keep = jnp.exp2((old - new) * EXP_SCALE)
            mixed = acc_in[rows, :] * jnp.concatenate([keep, keep], axis=1) + mixed
        if last:
            rest[0][rows, :] = (mixed[:, :HD] / mixed[:, HD:]).astype(rest[0].dtype)
        else:
            rest[0][rows, :] = mixed
            rest[1][rows, :] = new

    scores = scores_of(0)
    for start in range(0, tokens, step):
        following = scores_of(start + step) if start + step < tokens else None
        finish(start, scores)
        scores = following


def attend(flags, queries, tiles, gates, state=None, last=False, part=None, cost=32):
    channels = queries.shape[1]
    tokens = queries.shape[0] if part is None else queries.shape[0] // 2
    heads = channels // HD
    span = tiles[0].shape[1]

    def rows_spec(array, width):
        block = 0 if part is None or array.shape[0] == tokens else part
        return pl.BlockSpec((tokens, width), lambda h: (block, h))

    tile_spec = pl.BlockSpec((2, span, HD), lambda h: (0, 0, h))
    in_specs = [pl.BlockSpec(memory_space=pltpu.SMEM), rows_spec(queries, HD)] + [tile_spec] * len(tiles)
    args = [flags, queries, *tiles]
    if state is not None:
        in_specs += [rows_spec(state[0], 2 * HD), rows_spec(state[1], HD)]
        args += list(state)
    if last:
        out_shape = jax.ShapeDtypeStruct((tokens, channels), jnp.bfloat16)
        out_specs = rows_spec(out_shape, HD)
    else:
        out_shape = [
            jax.ShapeDtypeStruct((tokens, 2 * channels), jnp.float32),
            jax.ShapeDtypeStruct((tokens, channels), jnp.float32),
        ]
        out_specs = [rows_spec(out_shape[0], 2 * HD), rows_spec(out_shape[1], HD)]
    step = 256 if tokens % 256 == 0 else 192
    pairs = len(tiles) * heads * tokens * span
    return pl.pallas_call(
        functools.partial(attend_kernel, tuple(gates), state is None, last, step),
        out_shape=out_shape,
        grid=(heads,),
        in_specs=in_specs,
        out_specs=out_specs,
        compiler_params=pltpu.CompilerParams(vmem_limit_bytes=48 * 1024 * 1024),
        cost_estimate=pl.CostEstimate(flops=pairs * cost, bytes_accessed=1024, transcendentals=0),
    )(*args)


def body(queries, keys_values, out_weight):
    frames, rows, cols, channels = queries.shape
    tokens = frames * rows * cols
    half = channels // 2
    ha_count, wa_count = lax.axis_size("ha"), lax.axis_size("wa")
    ha, wa, ta = lax.axis_index("ha"), lax.axis_index("wa"), lax.axis_index("ta")
    odd = lax.rem(ha, 2)

    q_all = queries.reshape(tokens, channels)
    kv_all = keys_values.reshape(2, tokens, channels)
    keep_at, send_at = odd * half, (1 - odd) * half

    swap_pairs = [(i, i ^ 1) for i in range(ha_count)]
    native_pairs = [(i, (i + (2 if i % 2 else -2)) % ha_count) for i in range(ha_count)]
    swapped_pairs = [(i, (i + (-2 if i % 2 else 2)) % ha_count) for i in range(ha_count)]
    down_pairs = [(i, (i + 1) % wa_count) for i in range(wa_count)]
    up_pairs = [((i + 1) % wa_count, i) for i in range(wa_count)]

    def above_below(cells):
        return lax.ppermute(cells, "wa", down_pairs), lax.ppermute(cells, "wa", up_pairs)

    above, below = wa > 0, wa < wa_count - 1
    low, high = ha >= 2, ha < ha_count - 2
    far_partner = jnp.where(odd == 1, low, high)
    far_native = jnp.where(odd == 1, high, low)
    flags = jnp.stack(
        [above, below, far_partner, far_partner & above, far_partner & below,
         far_native, far_native & above, far_native & below]
    ).astype(jnp.int32)

    kv_send = lax.dynamic_slice_in_dim(kv_all, send_at, half, 2)
    kv_own = lax.dynamic_slice_in_dim(kv_all, keep_at, half, 2)
    q_send = lax.dynamic_slice_in_dim(q_all, send_at, half, 1)
    q_own = lax.dynamic_slice_in_dim(q_all, keep_at, half, 1)

    core, x_hi = lax.rem(ta, 2), ta // 2
    width = out_weight.shape[1] // lax.axis_size("ta")
    ordered = jnp.concatenate(
        [lax.dynamic_slice_in_dim(out_weight, at, half, 0) for at in (keep_at, send_at)], axis=0
    )

    def weight_of(for_core):
        groups = (2 * (1 - x_hi) + for_core, 2 * x_hi + for_core)
        return jnp.concatenate(
            [lax.dynamic_slice_in_dim(ordered, group * width, width, 1) for group in groups], axis=1
        )

    weight_send, weight_keep = weight_of(1 - core), weight_of(core)

    kv_pair = lax.ppermute(kv_send, "ha", swap_pairs)
    own_up, own_down = above_below(kv_own)
    far_p = lax.ppermute(kv_own, "ha", native_pairs)
    flags, weight_send, weight_keep = lax.optimization_barrier((flags, weight_send, weight_keep))
    state_n = attend(flags, q_own, [kv_own], [None])
    kv_pair, q_send, state_n = lax.optimization_barrier((kv_pair, q_send, state_n))
    q_pair = lax.ppermute(q_send, "ha", swap_pairs)
    pair_up, pair_down = above_below(kv_pair)
    far_n = lax.ppermute(kv_pair, "ha", swapped_pairs)
    far_p_up = lax.ppermute(own_up, "ha", native_pairs)
    far_p_down = lax.ppermute(own_down, "ha", native_pairs)
    state_n = attend(flags, q_own, [kv_pair, own_up, own_down], [None, 0, 1], state_n, cost=COST2)
    q_pair, state_n = lax.optimization_barrier((q_pair, state_n))
    state_p = attend(flags, q_pair, [kv_own, kv_pair, own_up, own_down, far_p], [None, None, 0, 1, 2])
    far_n, state_p = lax.optimization_barrier((far_n, state_p))
    far_n_up, far_n_down = above_below(far_n)
    state_p = attend(flags, q_pair, [pair_up, pair_down], [0, 1], state_p)
    state_n, state_p = lax.optimization_barrier((state_n, state_p))
    first_n = attend(flags, q_own, [pair_up, pair_down, far_n], [0, 1, 5], state_n, part=0)
    state_p, first_n, state_n = lax.optimization_barrier((state_p, first_n, state_n))
    backs = []
    for part in (0, 1):
        out_p = attend(flags, q_pair, [far_p_up, far_p_down], [3, 4], state_p, last=True, part=part)
        if part == 0:
            state_p, out_p = lax.optimization_barrier((state_p, out_p))
        else:
            first_n, state_n, out_p = lax.optimization_barrier((first_n, state_n, out_p))
        backs.append(lax.ppermute(out_p, "ha", swap_pairs))
    out_0 = attend(flags, q_own, [far_n_up, far_n_down], [6, 7], first_n, last=True, part=0)

    core_pairs = [(i, i ^ 1) for i in range(4)]
    hi_pairs = [(i, i ^ 2) for i in range(4)]

    def project(out_n, back):
        attention = jnp.concatenate([out_n, back], axis=1)
        sent = jnp.dot(attention, weight_send, preferred_element_type=jnp.float32).astype(jnp.bfloat16)
        taken = lax.ppermute(sent, "ta", core_pairs)
        kept = jnp.dot(attention, weight_keep, preferred_element_type=jnp.float32)
        away = (kept[:, :width] + taken[:, :width].astype(jnp.float32)).astype(jnp.bfloat16)
        return away, kept[:, width:] + taken[:, width:].astype(jnp.float32)

    away_0, home_0 = project(out_0, backs[0])
    away_0, state_n = lax.optimization_barrier((away_0, state_n))
    far_0 = lax.ppermute(away_0, "ta", hi_pairs)
    out_1 = attend(
        flags, q_own, [pair_up, pair_down, far_n, far_n_up, far_n_down], [0, 1, 5, 6, 7], state_n,
        last=True, part=1,
    )
    far_0, out_1 = lax.optimization_barrier((far_0, out_1))
    away_1, home_1 = project(out_1, backs[1])
    far_1 = lax.ppermute(away_1, "ta", hi_pairs)
    result = jnp.concatenate(
        [home_0 + far_0.astype(jnp.float32), home_1 + far_1.astype(jnp.float32)], axis=0
    )
    return result.astype(jnp.bfloat16).reshape(frames, rows, cols, width)


def solution(mesh):
    return jax.shard_map(
        body,
        mesh=mesh,
        in_specs=(P(None, "wa", "ha", "ta"), P(None, None, "wa", "ha", "ta"), P("ta", None)),
        out_specs=P(None, "wa", "ha", "ta"),
        check_vma=False,
    )
```

time: 177 us -> 160 us (0.904)
  waiting for transfers between devices: 60.3 us -> 45.6 us
  matrix products: 11 us -> 4.31 us
  other arithmetic: 3.08 us -> 8.09 us
  Pallas kernels: 59.1 us -> 62.7 us
  local copies, waits for them, and re-layouts: 12.4 us -> 9.45 us
    ppermute x1, waiting for transfers between devices: 23.2 us -> 0.01 us  [body(): far_p_up = lax.ppermute(own_up, 'ha', native_pairs)]
    ppermute x5 -> x7, waiting for transfers between devices: 24 us -> 35.1 us  [the longest x1 14.4 us: body(): far_1 = lax.ppermute(away_1, 'ta', hi_pairs)]
    concatenate x0 -> x3, other arithmetic: none -> 7.22 us  [the longest x1 3.59 us: weight_of(): jnp.concatenate([lax.dynamic_slice_in_dim(ordered, group * width, width,...]
    dot_general x4, matrix products: 11 us -> 4.31 us  [the longest x2 2.16 us: project(): jnp.dot(attention, weight_send, preferred_element_type=jnp.float32)]
    pallas_call x7 -> x9, Pallas kernels: 59.1 us -> 62.7 us  [attend(): pl.pallas_call(functools.partial(attend_kernel, tuple(gates), state is No...]
    convert_element_type x1 -> x2, other arithmetic: 3.07 us -> 0.38 us  [project(): (kept[:, :width] + taken[:, :width].astype(jnp.float32)).astype(jnp.bfloa...]
    ppermute x1, waiting for transfers between devices: 13.1 us -> 10.4 us  [body(): kv_pair = lax.ppermute(kv_send, 'ha', swap_pairs)]
    dynamic_slice x1, local copies, waits for them, and re-layouts: 4.85 us -> 2.7 us  [body(): lax.dynamic_slice_in_dim(out_weight, at, half, 0)]
  transfers between devices with their start and end apart: 16 -> 18, of which waited for: 3 -> 7; matrix products, arithmetic and copies ran while one was open for 8% -> 7% of each run, Pallas kernels for 33% -> 39%
where the time goes in v2:
time: 160 us
  Pallas kernels  62.7 us (39%)
  waiting for transfers between devices  45.6 us (28%)
  starting transfers between devices  29.4 us (18%)
  local copies, waits for them, and re-layouts  9.45 us (6%)
  other arithmetic  8.09 us (5%)
  matrix products  4.31 us (3%)
    pallas_call x9, Pallas kernels, attend(): pl.pallas_call(functools.partial(attend_kernel, tuple(gates), state is No...  62.7 us
    ppermute x1, waiting for transfers between devices, body(): far_1 = lax.ppermute(away_1, 'ta', hi_pairs)  14.4 us
    ppermute x1, waiting for transfers between devices, body(): kv_pair = lax.ppermute(kv_send, 'ha', swap_pairs)  10.4 us
    ppermute x2, waiting for transfers between devices, body(): backs.append(lax.ppermute(out_p, 'ha', swap_pairs))  7.16 us
    ppermute x1, waiting for transfers between devices, body(): q_pair = lax.ppermute(q_send, 'ha', swap_pairs)  6.95 us
    ppermute x2, starting transfers between devices, project(): taken = lax.ppermute(sent, 'ta', core_pairs)  5.7 us
    ppermute x3, starting transfers between devices, above_below(): lax.ppermute(cells, 'wa', up_pairs)  5.67 us
    ppermute x1, waiting for transfers between devices, body(): far_0 = lax.ppermute(away_0, 'ta', hi_pairs)  3.83 us
  transfers between devices with their start and end apart: 18, of which 7 were waited for; matrix products, arithmetic and copies ran while one was open for 7% of the time, Pallas kernels for 39%

profile of v2, /device:TPU:1, one launch (start us, length us, event | category | flops | bytes accessed | tf_op | source)
XLA Modules:
  0.0 159.8 jit_solution(17130765093659639880)
XLA Ops:
  0.0 2.9 %constant_dynamic-slice_fusion = (bf16[2,768,384]{2,1,0:T(8,128)(2,1)S(1)}, bf16[2,768,384]{2,1,0:T(8,128)(2,1)}) fusion(bf16[2,768,768]{2,1,0:T(8,128)(2,1)} %bitcast.17, s32[]{:T(128)S(6)} %select_n.36, s32[]{:T(128)S(6)} %select_n.37), kind=kLoop, calls=%fused_computation.31 | loop fusion | bytes 4718600 | tf_op jit(solution)/shard_map/dynamic_slice | solution.py:141
  2.9 2.1 %collective-permute-start.3 = (bf16[2,768,384]{2,1,0:T(8,128)(2,1)S(1)}, bf16[2,768,384]{2,1,0:T(8,128)(2,1)}, u32[]{:S(2)}, u32[]{:S(2)}) collective-permute-start(bf16[2,768,384]{2,1,0:T(8,128)(2,1)S(1)} %get-tuple-element.103.refs_2_), channel_id=1, source_target_pairs={{0,4},{4,8},{8,12},{12,0},{1,5},{5,9},{9,13},{13,1},{2,6},{6,10},{... | collective-permute-start | bytes 3538952 | tf_op jit(solution)/shard_map/ppermute | solution.py:129
  5.0 1.4 collective-permute-start.4
  6.4 3.8 %collective-permute-start.5 = (bf16[2,768,384]{2,1,0:T(8,128)(2,1)S(1)}, bf16[2,768,384]{2,1,0:T(8,128)(2,1)}, u32[]{:S(2)}, u32[]{:S(2)}) collective-permute-start(bf16[2,768,384]{2,1,0:T(8,128)(2,1)S(1)} %get-tuple-element.103.refs_2_), channel_id=1, source_target_pairs={{0,96},{16,48},{32,0},{48,80},{64,32},{80,112},{96,64},{112,16},{1... | collective-permute-start | bytes 3538952 | tf_op jit(solution)/shard_map/ppermute | solution.py:161
  10.2 2.7 %constant_dynamic-slice_fusion.4 = (bf16[384,3072]{1,0:T(8,128)(2,1)S(1)}, bf16[384,3072]{1,0:T(8,128)(2,1)S(1)}) fusion(bf16[768,3072]{1,0:T(8,128)(2,1)} %param.5, s32[]{:T(128)S(6)} %select_n.37, s32[]{:T(128)S(6)} %select_n.36), kind=kLoop, calls=%fused_computation.35 | loop fusion | bytes 9437192 | tf_op jit(solution)/shard_map/dynamic_slice | solution.py:148
  12.9 2.5 %fusion.3 = (bf16[768,768]{1,0:T(8,128)(2,1)}, bf16[768,768]{1,0:T(8,128)(2,1)}, bf16[768,768]{1,0:T(8,128)(2,1)}, bf16[768,768]{1,0:T(8,128)(2,1)}) fusion(s32[]{:T(128)S(6)} %select_n.41, bf16[384,3072]{1,0:T(8,128)(2,1)S(1)} %get-tuple-element.102, bf16[384,3072]{1,0:T(8,128)(2,1)S(1)} %get-tuple-element.101, s32[]{:T(128)S(6)} %select_n.39, ...), kind=kLoop, calls=%fused_computation.15 | loop fusion | flops 9437184 | bytes 9437200 | tf_op jit(solution)/shard_map/concatenate | solution.py:147
  15.6 3.6 %pad_maximum_fusion = (bf16[768,1536]{1,0:T(8,128)(2,1)}, bf16[768,1536]{1,0:T(8,128)(2,1)S(1)}) fusion(bf16[768,768]{1,0:T(8,128)(2,1)} %get-tuple-element.99, bf16[768,768]{1,0:T(8,128)(2,1)} %get-tuple-element.98, bf16[768,768]{1,0:T(8,128)(2,1)} %get-tuple-element.100, bf16[768,768]{1,0:T(8,128)(2,1)} %get-tuple-element.97), kind=kLoop, calls=%fused_computation.10 | loop fusion | flops 9437184 | bytes 9437184 | tf_op jit(solution)/shard_map/concatenate | solution.py:153
  19.3 4.1 %shard_map.37 = (f32[768,768]{1,0:T(8,128)S(1)}, f32[768,384]{1,0:T(8,128)S(1)}) custom-call(s32[8]{0:T(128)S(1)} %convert_element_type.38.refs_0_, bf16[768,384]{1,0:T(8,128)(2,1)S(1)} %get-tuple-element.105.refs_1_, bf16[2,768,384]{2,1,0:T(8,128)(2,1)S(1)} %get-tuple-element.103.refs_2_), custom_call_target="tpu_custom_call" | custom-call | flops 56623104 | bytes 1024 | tf_op jit(solution)/shard_map/pallas_call | solution.py:99
  23.4 1.4 copy-done.3
  26.0 10.4 %collective-permute-done.refs_2_.refs_3_ = bf16[2,768,384]{2,1,0:T(8,128)(2,1)S(1)} collective-permute-done((bf16[2,768,384]{2,1,0:T(8,128)(2,1)}, bf16[2,768,384]{2,1,0:T(8,128)(2,1)S(1)}, u32[]{:S(2)}, u32[]{:S(2)}) %collective-permute-start) | collective-permute-done | bytes 1179680 | tf_op jit(solution)/shard_map/ppermute | solution.py:159
  36.4 1.6 %collective-permute-start.2 = (bf16[768,384]{1,0:T(8,128)(2,1)S(1)}, bf16[768,384]{1,0:T(8,128)(2,1)S(1)}, u32[]{:S(2)}, u32[]{:S(2)}) collective-permute-start(bf16[768,384]{1,0:T(8,128)(2,1)S(1)} %get-tuple-element.55), channel_id=1, source_target_pairs={{0,16},{16,0},{32,48},{48,32},{64,80},{80,64},{96,112},{112,96},{1... | collective-permute-start | bytes 1769480 | tf_op jit(solution)/shard_map/ppermute | solution.py:165
  38.0 2.7 %collective-permute-start.9 = (bf16[2,768,384]{2,1,0:T(8,128)(2,1)S(1)}, bf16[2,768,384]{2,1,0:T(8,128)(2,1)S(1)}, u32[]{:S(2)}, u32[]{:S(2)}) collective-permute-start(bf16[2,768,384]{2,1,0:T(8,128)(2,1)S(1)} %collective-permute-done.refs_2_.refs_3_), channel_id=1, source_target_pairs={{4,0},{8,4},{12,8},{0,12},{5,1},{9,5},{13,9},{1,13},{6,2},{10,6},{... | collective-permute-start | bytes 3538952 | tf_op jit(solution)/shard_map/ppermute | solution.py:129
  41.9 7.0 %collective-permute-done.2.refs_1_ = bf16[768,384]{1,0:T(8,128)(2,1)S(1)} collective-permute-done((bf16[768,384]{1,0:T(8,128)(2,1)S(1)}, bf16[768,384]{1,0:T(8,128)(2,1)S(1)}, u32[]{:S(2)}, u32[]{:S(2)}) %collective-permute-start.2) | collective-permute-done | bytes 589856 | tf_op jit(solution)/shard_map/ppermute | solution.py:165
  48.8 2.1 %collective-permute-start.11 = (bf16[2,768,384]{2,1,0:T(8,128)(2,1)S(1)}, bf16[2,768,384]{2,1,0:T(8,128)(2,1)S(1)}, u32[]{:S(2)}, u32[]{:S(2)}) collective-permute-start(bf16[2,768,384]{2,1,0:T(8,128)(2,1)S(1)} %collective-permute-done.4.refs_4_.refs_5_), channel_id=1, source_target_pairs={{0,96},{16,48},{32,0},{48,80},{64,32},{80,112},{96,64},{112,16},{1... | collective-permute-start | bytes 3538952 | tf_op jit(solution)/shard_map/ppermute | solution.py:169
  51.0 9.7 %shard_map.38 = (f32[768,768]{1,0:T(8,128)}, f32[768,384]{1,0:T(8,128)S(1)}) custom-call(s32[8]{0:T(128)S(1)} %convert_element_type.38.refs_0_, bf16[768,384]{1,0:T(8,128)(2,1)S(1)} %get-tuple-element.105.refs_1_, bf16[2,768,384]{2,1,0:T(8,128)(2,1)S(1)} %collective-permute-done.refs_2_.refs_3_, bf16[2,768,384]{2,1,0:T(8,128)(2,1)} %collective-permute-done.3.refs_3_.refs_4_, ...), custom_call_target="tpu_custom_call" | custom-call | flops 5435817984 | bytes 1024 | tf_op jit(solution)/shard_map/pallas_call | solution.py:99
  61.7 13.5 %shard_map.39 = (f32[768,768]{1,0:T(8,128)}, f32[768,384]{1,0:T(8,128)S(1)}) custom-call(s32[8]{0:T(128)S(1)} %convert_element_type.38.refs_0_, bf16[768,384]{1,0:T(8,128)(2,1)S(1)} %collective-permute-done.2.refs_1_, bf16[2,768,384]{2,1,0:T(8,128)(2,1)S(1)} %get-tuple-element.103.refs_2_, bf16[2,768,384]{2,1,0:T(8,128)(2,1)S(1)} %collective-permute-done.refs_2_.refs_3_, ...), custom_call_target="tpu_custom_call" | custom-call | flops 283115520 | bytes 1024 | tf_op jit(solution)/shard_map/pallas_call | solution.py:99
  76.4 1.6 collective-permute-start.7
  78.0 7.7 %shard_map.40 = (f32[768,768]{1,0:T(8,128)}, f32[768,384]{1,0:T(8,128)S(1)}) custom-call(s32[8]{0:T(128)S(1)} %convert_element_type.38.refs_0_, bf16[768,384]{1,0:T(8,128)(2,1)S(1)} %collective-permute-done.2.refs_1_, bf16[2,768,384]{2,1,0:T(8,128)(2,1)S(1)} %collective-permute-done.8.refs_2_, bf16[2,768,384]{2,1,0:T(8,128)(2,1)S(1)} %collective-permute-done.9.refs_3_, ...), custom_call_target="tpu_custom_call" | custom-call | flops 113246208 | bytes 1024 | tf_op jit(solution)/shard_map/pallas_call | solution.py:99
  85.7 5.9 %shard_map.41 = (f32[384,768]{1,0:T(8,128)S(1)}, f32[384,384]{1,0:T(8,128)S(1)}) custom-call(s32[8]{0:T(128)S(1)} %convert_element_type.38.refs_0_, bf16[768,384]{1,0:T(8,128)(2,1)S(1)} %get-tuple-element.105.refs_1_, bf16[2,768,384]{2,1,0:T(8,128)(2,1)S(1)} %collective-permute-done.8.refs_2_, bf16[2,768,384]{2,1,0:T(8,128)(2,1)S(1)} %collective-permute-done.9.refs_3_, ...), custom_call_target="tpu_custom_call" | custom-call | flops 84934656 | bytes 1024 | tf_op jit(solution)/shard_map/pallas_call | solution.py:99
  91.6 4.6 %shard_map.42 = bf16[384,384]{1,0:T(8,128)(2,1)S(1)} custom-call(s32[8]{0:T(128)S(1)} %convert_element_type.38.refs_0_, bf16[768,384]{1,0:T(8,128)(2,1)S(1)} %collective-permute-done.2.refs_1_, bf16[2,768,384]{2,1,0:T(8,128)(2,1)S(1)} %collective-permute-done.10.refs_2_, bf16[2,768,384]{2,1,0:T(8,128)(2,1)S(1)} %collective-permute-done.11.refs_3_, ...), custom_call_target="tpu_custom_call" | custom-call | flops 56623104 | bytes 1024 | tf_op jit(solution)/shard_map/pallas_call | solution.py:99
  96.8 4.6 %shard_map.43 = bf16[384,384]{1,0:T(8,128)(2,1)S(1)} custom-call(s32[8]{0:T(128)S(1)} %convert_element_type.38.refs_0_, bf16[768,384]{1,0:T(8,128)(2,1)S(1)} %collective-permute-done.2.refs_1_, bf16[2,768,384]{2,1,0:T(8,128)(2,1)S(1)} %collective-permute-done.10.refs_2_, bf16[2,768,384]{2,1,0:T(8,128)(2,1)S(1)} %collective-permute-done.11.refs_3_, ...), custom_call_target="tpu_custom_call" | custom-call | flops 56623104 | bytes 1024 | tf_op jit(solution)/shard_map/pallas_call | solution.py:99
  101.5 4.2 %shard_map.44 = bf16[384,384]{1,0:T(8,128)(2,1)S(1)} custom-call(s32[8]{0:T(128)S(1)} %convert_element_type.38.refs_0_, bf16[768,384]{1,0:T(8,128)(2,1)S(1)} %get-tuple-element.105.refs_1_, bf16[2,768,384]{2,1,0:T(8,128)(2,1)S(1)} %collective-permute-done.6.refs_2_.refs_5_, bf16[2,768,384]{2,1,0:T(8,128)(2,1)S(1)} %collective-permute-done.7.refs_3_.refs_6_, ...), custom_call_target="tpu_custom_call" | custom-call | flops 56623104 | bytes 1024 | tf_op jit(solution)/shard_map/pallas_call | solution.py:99
  106.8 4.4 %collective-permute-start.13 = (bf16[384,1536]{1,0:T(8,128)(2,1)S(1)}, bf16[384,1536]{1,0:T(8,128)(2,1)S(1)}, u32[]{:S(2)}, u32[]{:S(2)}) collective-permute-start(bf16[384,1536]{1,0:T(8,128)(2,1)S(1)} %convolution_convert_fusion.1), channel_id=1, source_target_pairs={{0,1},{1,0},{2,3},{3,2},{4,5},{5,4},{6,7},{7,6},{8,9},{9,8},{10,11... | collective-permute-start | bytes 3538952 | tf_op jit(solution)/shard_map/ppermute | solution.py:195
  112.4 1.4 collective-permute-done.13
  113.9 2.8 %collective-permute-start.14 = (bf16[384,768]{1,0:T(8,128)(2,1)S(1)}, bf16[384,768]{1,0:T(8,128)(2,1)S(1)}, u32[]{:S(2)}, u32[]{:S(2)}) collective-permute-start(bf16[384,768]{1,0:T(8,128)(2,1)S(1)} %fusion.7), channel_id=1, source_target_pairs={{0,2},{1,3},{2,0},{3,1},{4,6},{5,7},{6,4},{7,5},{8,10},{9,11},{10,... | collective-permute-start | bytes 1769480 | tf_op jit(solution)/shard_map/ppermute | solution.py:202
  117.9 8.4 %shard_map.45 = bf16[384,384]{1,0:T(8,128)(2,1)S(1)} custom-call(s32[8]{0:T(128)S(1)} %convert_element_type.38.refs_0_, bf16[768,384]{1,0:T(8,128)(2,1)S(1)} %get-tuple-element.105.refs_1_, bf16[2,768,384]{2,1,0:T(8,128)(2,1)S(1)} %collective-permute-done.8.refs_2_, bf16[2,768,384]{2,1,0:T(8,128)(2,1)S(1)} %collective-permute-done.9.refs_3_, ...), custom_call_target="tpu_custom_call" | custom-call | flops 141557760 | bytes 1024 | tf_op jit(solution)/shard_map/pallas_call | solution.py:99
  126.2 3.8 %collective-permute-done.14 = bf16[384,768]{1,0:T(8,128)(2,1)S(1)} collective-permute-done((bf16[384,768]{1,0:T(8,128)(2,1)S(1)}, bf16[384,768]{1,0:T(8,128)(2,1)S(1)}, u32[]{:S(2)}, u32[]{:S(2)}) %collective-permute-start.14) | collective-permute-done | bytes 589856 | tf_op jit(solution)/shard_map/ppermute | solution.py:202
  130.1 7.2 %collective-permute-done.15 = bf16[384,384]{1,0:T(8,128)(2,1)S(1)} collective-permute-done((bf16[384,384]{1,0:T(8,128)(2,1)S(1)}, bf16[384,384]{1,0:T(8,128)(2,1)S(1)}, u32[]{:S(2)}, u32[]{:S(2)}) %collective-permute-start.15) | collective-permute-done | bytes 294944 | tf_op jit(solution)/shard_map/ppermute | solution.py:186
  138.4 1.3 collective-permute-start.16
  140.8 1.4 collective-permute-done.16
  142.3 1.5 collective-permute-start.17
  144.1 14.4 %collective-permute-done.17 = bf16[384,768]{1,0:T(8,128)(2,1)S(1)} collective-permute-done((bf16[384,768]{1,0:T(8,128)(2,1)S(1)}, bf16[384,768]{1,0:T(8,128)(2,1)S(1)}, u32[]{:S(2)}, u32[]{:S(2)}) %collective-permute-start.17) | collective-permute-done | bytes 589856 | tf_op jit(solution)/shard_map/ppermute | solution.py:209
  (47 shorter events, 12.9 us)
Async XLA Ops:
  2.9 33.5 %collective-permute-start.3 = (bf16[2,768,384]{2,1,0:T(8,128)(2,1)S(1)}, bf16[2,768,384]{2,1,0:T(8,128)(2,1)}, u32[]{:S(2)}, u32[]{:S(2)}) collective-permute-start(bf16[2,768,384]{2,1,0:T(8,128)(2,1)S(1)} %get-tuple-element.103.refs_2_), channel_id=1, source_target_pairs={{0,4},{4,8},{8,12},{12,0},{1,5},{5,9},{9,13},{13,1},{2,6},{6,10},{... | collective-permute-start | bytes 3538952 | tf_op jit(solution)/shard_map/ppermute | solution.py:129
  5.0 33.0 %collective-permute-start.4 = (bf16[2,768,384]{2,1,0:T(8,128)(2,1)S(1)}, bf16[2,768,384]{2,1,0:T(8,128)(2,1)S(1)}, u32[]{:S(2)}, u32[]{:S(2)}) collective-permute-start(bf16[2,768,384]{2,1,0:T(8,128)(2,1)S(1)} %get-tuple-element.103.refs_2_), channel_id=1, source_target_pairs={{4,0},{8,4},{12,8},{0,12},{5,1},{9,5},{13,9},{1,13},{6,2},{10,6},{... | collective-permute-start | bytes 3538952 | tf_op jit(solution)/shard_map/ppermute | solution.py:129
  6.4 34.3 %collective-permute-start.5 = (bf16[2,768,384]{2,1,0:T(8,128)(2,1)S(1)}, bf16[2,768,384]{2,1,0:T(8,128)(2,1)}, u32[]{:S(2)}, u32[]{:S(2)}) collective-permute-start(bf16[2,768,384]{2,1,0:T(8,128)(2,1)S(1)} %get-tuple-element.103.refs_2_), channel_id=1, source_target_pairs={{0,96},{16,48},{32,0},{48,80},{64,32},{80,112},{96,64},{112,16},{1... | collective-permute-start | bytes 3538952 | tf_op jit(solution)/shard_map/ppermute | solution.py:161
  10.2 26.2 %collective-permute-start = (bf16[2,768,384]{2,1,0:T(8,128)(2,1)}, bf16[2,768,384]{2,1,0:T(8,128)(2,1)S(1)}, u32[]{:S(2)}, u32[]{:S(2)}) collective-permute-start(bf16[2,768,384]{2,1,0:T(8,128)(2,1)} %get-tuple-element.104), channel_id=1, source_target_pairs={{0,16},{16,0},{32,48},{48,32},{64,80},{80,64},{96,112},{112,96},{1... | collective-permute-start | bytes 3538952 | tf_op jit(solution)/shard_map/ppermute | solution.py:159
  15.6 3.6 %copy-start.7 = (bf16[12,8,8,768]{3,2,1,0:T(8,128)(2,1)S(1)}, bf16[12,8,8,768]{3,2,1,0:T(8,128)(2,1)}, u32[]{:S(2)}) copy-start(bf16[12,8,8,768]{3,2,1,0:T(8,128)(2,1)} %param.3) | copy-start | bytes 3538948
  23.4 1.5 copy-start.3
  24.9 1.1 copy-start.4
  36.4 38.8 %collective-permute-start.1 = (bf16[2,768,384]{2,1,0:T(8,128)(2,1)S(1)}, bf16[2,768,384]{2,1,0:T(8,128)(2,1)S(1)}, u32[]{:S(2)}, u32[]{:S(2)}) collective-permute-start(bf16[2,768,384]{2,1,0:T(8,128)(2,1)S(1)} %collective-permute-done.refs_2_.refs_3_), channel_id=1, source_target_pairs={{0,32},{16,112},{32,64},{48,16},{64,96},{80,48},{96,0},{112,80},{1... | collective-permute-start | bytes 3538952 | tf_op jit(solution)/shard_map/ppermute | solution.py:167
  36.4 40.0 %collective-permute-start.8 = (bf16[2,768,384]{2,1,0:T(8,128)(2,1)S(1)}, bf16[2,768,384]{2,1,0:T(8,128)(2,1)S(1)}, u32[]{:S(2)}, u32[]{:S(2)}) collective-permute-start(bf16[2,768,384]{2,1,0:T(8,128)(2,1)S(1)} %collective-permute-done.refs_2_.refs_3_), channel_id=1, source_target_pairs={{0,4},{4,8},{8,12},{12,0},{1,5},{5,9},{9,13},{13,1},{2,6},{6,10},{... | collective-permute-start | bytes 3538952 | tf_op jit(solution)/shard_map/ppermute | solution.py:129
  36.4 12.4 %collective-permute-start.2 = (bf16[768,384]{1,0:T(8,128)(2,1)S(1)}, bf16[768,384]{1,0:T(8,128)(2,1)S(1)}, u32[]{:S(2)}, u32[]{:S(2)}) collective-permute-start(bf16[768,384]{1,0:T(8,128)(2,1)S(1)} %get-tuple-element.55), channel_id=1, source_target_pairs={{0,16},{16,0},{32,48},{48,32},{64,80},{80,64},{96,112},{112,96},{1... | collective-permute-start | bytes 1769480 | tf_op jit(solution)/shard_map/ppermute | solution.py:165
  38.0 22.6 %copy-start.2 = (bf16[2,768,384]{2,1,0:T(8,128)(2,1)}, bf16[2,768,384]{2,1,0:T(8,128)(2,1)S(1)}, u32[]{:S(2)}) copy-start(bf16[2,768,384]{2,1,0:T(8,128)(2,1)S(1)} %collective-permute-done.4.refs_4_.refs_5_) | copy-start | bytes 3538948
  38.0 39.9 %collective-permute-start.9 = (bf16[2,768,384]{2,1,0:T(8,128)(2,1)S(1)}, bf16[2,768,384]{2,1,0:T(8,128)(2,1)S(1)}, u32[]{:S(2)}, u32[]{:S(2)}) collective-permute-start(bf16[2,768,384]{2,1,0:T(8,128)(2,1)S(1)} %collective-permute-done.refs_2_.refs_3_), channel_id=1, source_target_pairs={{4,0},{8,4},{12,8},{0,12},{5,1},{9,5},{13,9},{1,13},{6,2},{10,6},{... | collective-permute-start | bytes 3538952 | tf_op jit(solution)/shard_map/ppermute | solution.py:129
  40.7 50.9 %collective-permute-start.10 = (bf16[2,768,384]{2,1,0:T(8,128)(2,1)}, bf16[2,768,384]{2,1,0:T(8,128)(2,1)S(1)}, u32[]{:S(2)}, u32[]{:S(2)}) collective-permute-start(bf16[2,768,384]{2,1,0:T(8,128)(2,1)} %collective-permute-done.3.refs_3_.refs_4_), channel_id=1, source_target_pairs={{0,96},{16,48},{32,0},{48,80},{64,32},{80,112},{96,64},{112,16},{1... | collective-permute-start | bytes 3538952 | tf_op jit(solution)/shard_map/ppermute | solution.py:168
  48.8 42.8 %collective-permute-start.11 = (bf16[2,768,384]{2,1,0:T(8,128)(2,1)S(1)}, bf16[2,768,384]{2,1,0:T(8,128)(2,1)S(1)}, u32[]{:S(2)}, u32[]{:S(2)}) collective-permute-start(bf16[2,768,384]{2,1,0:T(8,128)(2,1)S(1)} %collective-permute-done.4.refs_4_.refs_5_), channel_id=1, source_target_pairs={{0,96},{16,48},{32,0},{48,80},{64,32},{80,112},{96,64},{112,16},{1... | collective-permute-start | bytes 3538952 | tf_op jit(solution)/shard_map/ppermute | solution.py:169
  60.7 1.0 copy-start.1
  75.2 26.3 %collective-permute-start.6 = (bf16[2,768,384]{2,1,0:T(8,128)(2,1)S(1)}, bf16[2,768,384]{2,1,0:T(8,128)(2,1)S(1)}, u32[]{:S(2)}, u32[]{:S(2)}) collective-permute-start(bf16[2,768,384]{2,1,0:T(8,128)(2,1)S(1)} %collective-permute-done.1.refs_4_), channel_id=1, source_target_pairs={{0,4},{4,8},{8,12},{12,0},{1,5},{5,9},{9,13},{13,1},{2,6},{6,10},{... | collective-permute-start | bytes 3538952 | tf_op jit(solution)/shard_map/ppermute | solution.py:129
  76.4 25.1 %collective-permute-start.7 = (bf16[2,768,384]{2,1,0:T(8,128)(2,1)S(1)}, bf16[2,768,384]{2,1,0:T(8,128)(2,1)S(1)}, u32[]{:S(2)}, u32[]{:S(2)}) collective-permute-start(bf16[2,768,384]{2,1,0:T(8,128)(2,1)S(1)} %collective-permute-done.1.refs_4_), channel_id=1, source_target_pairs={{4,0},{8,4},{12,8},{0,12},{5,1},{9,5},{13,9},{1,13},{6,2},{10,6},{... | collective-permute-start | bytes 3538952 | tf_op jit(solution)/shard_map/ppermute | solution.py:129
  96.2 9.5 %collective-permute-start.12 = (bf16[384,384]{1,0:T(8,128)(2,1)S(1)}, bf16[384,384]{1,0:T(8,128)(2,1)S(1)}, u32[]{:S(2)}, u32[]{:S(2)}) collective-permute-start(bf16[384,384]{1,0:T(8,128)(2,1)S(1)} %shard_map.42), channel_id=1, source_target_pairs={{0,16},{16,0},{32,48},{48,32},{64,80},{80,64},{96,112},{112,96},{1... | collective-permute-start | bytes 884744 | tf_op jit(solution)/shard_map/ppermute | solution.py:186
  101.5 4.3 %copy-start.5 = (bf16[768,1536]{1,0:T(8,128)(2,1)S(1)}, bf16[768,1536]{1,0:T(8,128)(2,1)}, u32[]{:S(2)}) copy-start(bf16[768,1536]{1,0:T(8,128)(2,1)} %get-tuple-element.88) | copy-start | bytes 7077892
  101.5 4.2 %copy-start = (bf16[2,768,384]{2,1,0:T(8,128)(2,1)}, bf16[2,768,384]{2,1,0:T(8,128)(2,1)S(1)}, u32[]{:S(2)}) copy-start(bf16[2,768,384]{2,1,0:T(8,128)(2,1)S(1)} %collective-permute-done.7.refs_3_.refs_6_) | copy-start | bytes 3538948
  106.8 6.9 %collective-permute-start.13 = (bf16[384,1536]{1,0:T(8,128)(2,1)S(1)}, bf16[384,1536]{1,0:T(8,128)(2,1)S(1)}, u32[]{:S(2)}, u32[]{:S(2)}) collective-permute-start(bf16[384,1536]{1,0:T(8,128)(2,1)S(1)} %convolution_convert_fusion.1), channel_id=1, source_target_pairs={{0,1},{1,0},{2,3},{3,2},{4,5},{5,4},{6,7},{7,6},{8,9},{9,8},{10,11... | collective-permute-start | bytes 3538952 | tf_op jit(solution)/shard_map/ppermute | solution.py:195
  113.9 23.4 %copy-start.6 = (bf16[768,1536]{1,0:T(8,128)(2,1)S(1)}, bf16[768,1536]{1,0:T(8,128)(2,1)}, u32[]{:S(2)}) copy-start(bf16[768,1536]{1,0:T(8,128)(2,1)} %get-tuple-element.88) | copy-start | bytes 7077892
  113.9 16.1 %collective-permute-start.14 = (bf16[384,768]{1,0:T(8,128)(2,1)S(1)}, bf16[384,768]{1,0:T(8,128)(2,1)S(1)}, u32[]{:S(2)}, u32[]{:S(2)}) collective-permute-start(bf16[384,768]{1,0:T(8,128)(2,1)S(1)} %fusion.7), channel_id=1, source_target_pairs={{0,2},{1,3},{2,0},{3,1},{4,6},{5,7},{6,4},{7,5},{8,10},{9,11},{10,... | collective-permute-start | bytes 1769480 | tf_op jit(solution)/shard_map/ppermute | solution.py:202
  116.8 20.5 %collective-permute-start.15 = (bf16[384,384]{1,0:T(8,128)(2,1)S(1)}, bf16[384,384]{1,0:T(8,128)(2,1)S(1)}, u32[]{:S(2)}, u32[]{:S(2)}) collective-permute-start(bf16[384,384]{1,0:T(8,128)(2,1)S(1)} %shard_map.43), channel_id=1, source_target_pairs={{0,16},{16,0},{32,48},{48,32},{64,80},{80,64},{96,112},{112,96},{1... | collective-permute-start | bytes 884744 | tf_op jit(solution)/shard_map/ppermute | solution.py:186
  138.4 3.8 %collective-permute-start.16 = (bf16[384,1536]{1,0:T(8,128)(2,1)S(1)}, bf16[384,1536]{1,0:T(8,128)(2,1)S(1)}, u32[]{:S(2)}, u32[]{:S(2)}) collective-permute-start(bf16[384,1536]{1,0:T(8,128)(2,1)S(1)} %convolution_convert_fusion), channel_id=1, source_target_pairs={{0,1},{1,0},{2,3},{3,2},{4,5},{5,4},{6,7},{7,6},{8,9},{9,8},{10,11... | collective-permute-start | bytes 3538952 | tf_op jit(solution)/shard_map/ppermute | solution.py:195
  142.3 16.1 %collective-permute-start.17 = (bf16[384,768]{1,0:T(8,128)(2,1)S(1)}, bf16[384,768]{1,0:T(8,128)(2,1)S(1)}, u32[]{:S(2)}, u32[]{:S(2)}) collective-permute-start(bf16[384,768]{1,0:T(8,128)(2,1)S(1)} %fusion.4), channel_id=1, source_target_pairs={{0,2},{1,3},{2,0},{3,1},{4,6},{5,7},{6,4},{7,5},{8,10},{9,11},{10,... | collective-permute-start | bytes 1769480 | tf_op jit(solution)/shard_map/ppermute | solution.py:209
